TPU v7x, 32 devices: a whole 2x2x4 slice. The times are simulated.
32 devices in a mesh: cuts: 4 (over x, core), tile: 8 (over z, y).
Axes of the slice: x: 2, y: 2, z: 4, core: 2. Of those that a mesh axis runs over, the one named last changes fastest.
Arguments:
- acquired: bfloat16 [524288, 256], P(('cuts', 'tile')), may hold values from -6 to 6
- stencil: bfloat16 [2048, 1024], P('tile'), may hold values from -0.0390625 to 0.0390625
- send_slots: int32 [32, 8, 1280], P(('cuts', 'tile')), may hold values from 0 to 16383
- send_lines: int32 [32, 8, 1280], P(('cuts', 'tile')), may hold values from 0 to 1023
- send_counts: int32 [32, 8], P(('cuts', 'tile')), may hold values from 1 to 1280, as said below
- return_slots: int32 [32, 8, 128], P(('cuts', 'tile')), may hold values from 0 to 255
- return_counts: int32 [32, 8], P(('cuts', 'tile')), may hold values from 1 to 128, as said below
Outputs:
- field_out: bfloat16 [32, 256, 256], P(('cuts', 'tile'))
- returned: bfloat16 [256, 128, 256], P(('cuts', 'tile'))
Inputs may be any that keep to these rules, and one draw needn't show every extreme that they name: `send_counts`: some tile receives 1280 rows from every device. `return_counts`: some reader tile receives 128 lines from every owner.
All inputs are finite; a program needn't handle non-finite values.
Results may differ from a plain program's by a relative error of at most 0.00075.
Values may be sent and summed in bfloat16 or wider, within the bound.
A program may use at most 192 MiB of HBM per device.

v0:
```python
import jax
import jax.numpy as jnp
from jax import lax
from jax.sharding import PartitionSpec as P

NX = 256
NY = 256
TAPS = 4
ITERS = 2
ZDEV = 1


def with_halo(cells, sides, width):
    for axis, dim in sides:
        count = lax.axis_size(axis)
        ends = count - 1
        head = lax.slice_in_dim(cells, 0, width, axis=dim)
        tail = lax.slice_in_dim(cells, cells.shape[dim] - width, cells.shape[dim], axis=dim)
        cells = jnp.concatenate(
            [
                lax.ppermute(tail, axis, [(i, (i + 1) % count) for i in range(ends)]),
                cells,
                lax.ppermute(head, axis, [((i + 1) % count, i) for i in range(ends)]),
            ],
            axis=dim,
        )
    return cells


def local_sum(padded, inner):
    ypad = jnp.pad(inner, ((0, 0), (1, 1), (0, 0)))
    xpad = jnp.pad(inner, ((0, 0), (0, 0), (1, 1)))
    return padded[2:] + padded[:-2] + ypad[:, 2:] + ypad[:, :-2] + xpad[:, :, 2:] + xpad[:, :, :-2]


def line_sums(rows_block, lines_block, line_total):
    line_range = jnp.arange(line_total, dtype=jnp.int32)
    onehot = (line_range[:, None] == lines_block[None, :]).astype(jnp.bfloat16)
    return jnp.dot(onehot, rows_block, preferred_element_type=jnp.float32)


def apply_stencil(line_field, stencil):
    plane_total = line_field.shape[0] // NY
    product = jnp.dot(line_field, stencil.astype(jnp.float32), precision=lax.Precision.HIGHEST)
    product = product.reshape(plane_total, NY, TAPS, NX)
    accum_planes = product[:, :, 0, :]
    for shift_k in range(1, TAPS):
        accum_planes = accum_planes + jnp.roll(product[:, :, shift_k, :], shift_k, axis=1)
    return accum_planes


def local(acquired, stencil, send_slots, send_lines, send_counts, return_slots, return_counts):
    tile_count = lax.axis_size("tile")
    cut_count = lax.axis_size("cuts")
    slots = send_slots[0]
    line_ids = send_lines[0]
    counts = send_counts[0]
    slot_total = slots.shape[1]
    slot_index = jnp.arange(slot_total, dtype=jnp.int32)
    usable = slot_index[None, :] < counts[:, None]
    picked = jnp.take(acquired, slots.reshape(-1), axis=0).reshape(tile_count, slot_total, NX)
    picked = jnp.where(usable[:, :, None], picked, jnp.zeros_like(picked))
    line_ids = jnp.where(usable, line_ids, 0)
    group_lines = cut_count * ZDEV * NY
    arrived, arrived_lines = (
        lax.all_to_all(picked, "tile", split_axis=0, concat_axis=0, tiled=True),
        lax.all_to_all(line_ids, "tile", split_axis=0, concat_axis=0, tiled=True),
    )

    def add_source(carry_lines, source_item):
        rows_block, lines_block = source_item
        return (carry_lines + line_sums(rows_block, lines_block, group_lines), None)

    line_buffer = jnp.zeros((group_lines, NX), jnp.float32)
    line_buffer, _ = lax.scan(add_source, line_buffer, (arrived, arrived_lines))
    line_planes = line_buffer.reshape(cut_count * ZDEV, NY, NX)
    own_lines = lax.psum_scatter(line_planes, "cuts", scatter_dimension=0, tiled=True)
    smooth_field = apply_stencil(own_lines.reshape(ZDEV * NY, NX), stencil)
    for sweep in range(ITERS):
        padded = with_halo(smooth_field, ((("cuts", "tile"), 0),), 1)
        smooth_field = smooth_field + 0.15 * (local_sum(padded, smooth_field) - 6.0 * smooth_field)
    field_out = smooth_field.astype(jnp.bfloat16)
    read_ids = return_slots[0]
    read_counts = return_counts[0]
    read_total = read_ids.shape[1]
    flat_field = field_out.reshape(ZDEV * NY, NX)
    read_index = jnp.arange(read_total, dtype=jnp.int32)
    usable_back = read_index[None, :] < read_counts[:, None]
    own_range = jnp.arange(ZDEV * NY, dtype=jnp.int32)
    selector = (read_ids.reshape(-1)[:, None] == own_range[None, :]) & usable_back.reshape(-1)[
        :, None
    ]
    outgoing = jnp.dot(
        selector.astype(jnp.bfloat16), flat_field, preferred_element_type=jnp.float32
    )
    outgoing = outgoing.astype(jnp.bfloat16).reshape(tile_count, read_total, NX)
    returned = lax.all_to_all(outgoing, "tile", split_axis=0, concat_axis=0, tiled=True)
    return (field_out, returned)


def solution(mesh):
    in_specs = (
        P(("cuts", "tile"), None),
        P("tile", None),
        P(("cuts", "tile"), None, None),
        P(("cuts", "tile"), None, None),
        P(("cuts", "tile"), None),
        P(("cuts", "tile"), None, None),
        P(("cuts", "tile"), None),
    )
    out_specs = (P(("cuts", "tile"), None, None), P(("cuts", "tile"), None, None))
    return jax.shard_map(local, mesh=mesh, in_specs=in_specs, out_specs=out_specs, check_vma=False)
```

profile of v0, /device:TPU:0, one launch (start us, length us, event | category | flops | bytes accessed | tf_op | source)
XLA Modules:
  0.0 300.0 jit_solution(1868094592882958071)
XLA Ops:
  7.2 1.5 compare_select_fusion.1
  8.7 7.3 %all-to-all-start = ((s32[8,1,1280]{2,1,0:T(1,128)}), s32[8,1,1280]{2,1,0:T(1,128)S(1)}, u32[]{:S(2)}, u32[]{:S(2)}) async-start(s32[8,1,1280]{2,1,0:T(1,128)} %compare_select_fusion.1), calls=%async_computation | async-start | bytes 81920 | tf_op jit(solution)/shard_map/all_to_all | solution.py:67
  15.9 0.7 iota_compare_fusion.5
  16.7 0.8 compare_and_fusion
  17.5 0.8 copy.13
  18.4 43.0 %gather_fusion = bf16[10240,256]{1,0:T(8,128)(2,1)} fusion(bf16[16384,256]{1,0:T(8,128)(2,1)} %param.9, s32[10240]{0:T(1024)S(1)} %broadcast_clamp_fusion), kind=kCustom, calls=%fused_computation | custom fusion | bytes 10526720 | tf_op jit(solution)/shard_map/jit(_take)/gather | solution.py:61
  61.4 9.4 %select_select_fusion = bf16[8,1280,256]{2,1,0:T(8,128)(2,1)} fusion(bf16[8,1280,256]{2,1,0:T(8,128)(2,1)} %bitcast.53, pred[8,1280]{1,0:T(8,128)(4,1)S(1)} %compare_and_fusion, pred[8,1280]{1,0:T(8,128)(4,1)S(1)} %iota_compare_fusion.5), kind=kLoop, calls=%fused_computation.9 | loop fusion | flops 5242880 | bytes 10506240 | tf_op jit(solution)/shard_map/jit(_where)/select_n | solution.py:62
  70.7 0.0 all-to-all-done
  70.7 6.0 %all-to-all-start.1 = ((bf16[8,1280,256]{2,1,0:T(8,128)(2,1)}), bf16[8,1280,256]{2,1,0:T(8,128)(2,1)}, u32[]{:S(2)}, u32[]{:S(2)}) async-start(bf16[8,1280,256]{2,1,0:T(8,128)(2,1)} %select_select_fusion), calls=%async_computation.1 | async-start | bytes 10485760 | tf_op jit(solution)/shard_map/all_to_all | solution.py:66
  76.7 0.0 reduce-scatter.2.cloned.1.call-start
  76.8 115.1 %all-to-all-done.1 = bf16[8,1280,256]{2,1,0:T(8,128)(2,1)} async-done(((bf16[8,1280,256]{2,1,0:T(8,128)(2,1)}), bf16[8,1280,256]{2,1,0:T(8,128)(2,1)}, u32[]{:S(2)}, u32[]{:S(2)}) %all-to-all-start.1) | async-done | bytes 5242912 | tf_op jit(solution)/shard_map/all_to_all | solution.py:66
  191.9 0.0 copy-start.1
  191.9 19.0 %while.11 = (s32[]{:T(128)}, f32[1024,256]{1,0:T(8,128)S(1)}, s32[8,1280]{1,0:T(8,128)S(1)}, bf16[8,1280,256]{2,1,0:T(8,128)(2,1)}, s32[]{:T(128)}, /*index=5*/s32[]{:T(128)}) while((s32[]{:T(128)}, f32[1024,256]{1,0:T(8,128)S(1)}, s32[8,1280]{1,0:T(8,128)S(1)}, bf16[8,1280,256]{2,1,0:T(8,128)(2,1)}, s32[]{:T(128)}, ...), condition=%wide.region_1.2_spmd.clone, body=%wide.region_0.1_spmd.clone.sunk | while | flops 672923648 | bytes 2768467 | solution.py:75
  192.0 2.4 fusion.31
  194.4 2.3 fusion.31
  196.8 2.3 fusion.31
  199.1 2.3 fusion.31
  201.5 2.3 fusion.31
  203.9 2.3 fusion.31
  206.2 2.3 fusion.31
  208.6 2.3 fusion.31
  210.9 0.0 copy-start
  210.9 0.0 copy-start.4
  210.9 0.0 copy-start.3
  210.9 0.9 copy-done
  211.9 0.0 reduce-scatter.2.cloned.1.call-update
  211.9 0.0 copy-done.1
  211.9 0.2 copy.11
  212.1 23.9 %reduce-scatter.2.cloned.1.call-done = f32[1,256,256]{2,1,0:T(8,128)} async-done(((f32[4,256,256]{2,1,0:T(8,128)}), f32[1,256,256]{2,1,0:T(8,128)}) %reduce-scatter.2.cloned.1.call-update) | async-done | bytes 262160 | tf_op jit(solution)/shard_map/reduce_scatter | solution.py:77
  236.0 1.6 convolution_bitcast_fusion
  237.6 0.1 slice_bitcast_fusion
  237.7 0.1 fusion.23
  237.8 1.3 collective-permute-start
  239.1 4.6 %collective-permute-start.1 = (f32[1,256,256]{2,1,0:T(8,128)S(1)}, f32[1,256,256]{2,1,0:T(8,128)S(1)}, u32[]{:S(2)}, u32[]{:S(2)}) collective-permute-start(f32[1,256,256]{2,1,0:T(8,128)S(1)} %fusion.23), channel_id=1, source_target_pairs={{0,1},{1,2},{2,3},{3,4},{4,5},{5,6},{6,7},{7,8},{8,9},{9,10},{10,1... | collective-permute-start | bytes 786440 | tf_op jit(solution)/shard_map/ppermute | solution.py:21
  243.6 4.1 %collective-permute-done = f32[1,256,256]{2,1,0:T(8,128)S(1)} collective-permute-done((f32[1,256,256]{2,1,0:T(8,128)S(1)}, f32[1,256,256]{2,1,0:T(8,128)S(1)}, u32[]{:S(2)}, u32[]{:S(2)}) %collective-permute-start) | collective-permute-done | bytes 262176 | tf_op jit(solution)/shard_map/ppermute | solution.py:23
  247.7 5.4 %collective-permute-done.1 = f32[1,256,256]{2,1,0:T(8,128)S(1)} collective-permute-done((f32[1,256,256]{2,1,0:T(8,128)S(1)}, f32[1,256,256]{2,1,0:T(8,128)S(1)}, u32[]{:S(2)}, u32[]{:S(2)}) %collective-permute-start.1) | collective-permute-done | bytes 262176 | tf_op jit(solution)/shard_map/ppermute | solution.py:21
  253.1 0.2 fusion.14
  253.3 1.3 collective-permute-start.2
  254.7 5.0 %collective-permute-start.3 = (f32[1,256,256]{2,1,0:T(8,128)S(1)}, f32[1,256,256]{2,1,0:T(8,128)S(1)}, u32[]{:S(2)}, u32[]{:S(2)}) collective-permute-start(f32[1,256,256]{2,1,0:T(8,128)S(1)} %fusion.14), channel_id=1, source_target_pairs={{0,1},{1,2},{2,3},{3,4},{4,5},{5,6},{6,7},{7,8},{8,9},{9,10},{10,1... | collective-permute-start | bytes 786440 | tf_op jit(solution)/shard_map/ppermute | solution.py:21
  259.7 0.0 copy-done.4
  259.7 0.1 fusion.26
  259.8 2.5 collective-permute-done.2
  262.2 7.8 %collective-permute-done.3 = f32[1,256,256]{2,1,0:T(8,128)S(1)} collective-permute-done((f32[1,256,256]{2,1,0:T(8,128)S(1)}, f32[1,256,256]{2,1,0:T(8,128)S(1)}, u32[]{:S(2)}, u32[]{:S(2)}) %collective-permute-start.3) | collective-permute-done | bytes 262176 | tf_op jit(solution)/shard_map/ppermute | solution.py:21
  270.0 0.2 fusion.20
  270.2 0.0 copy-start.2
  270.2 0.0 copy-done.3
  270.2 0.5 convolution_convert_fusion
  270.7 21.6 %all_to_all.19 = bf16[8,128,256]{2,1,0:T(8,128)(2,1)S(1)} all-to-all(bf16[8,128,256]{2,1,0:T(8,128)(2,1)S(1)} %bitcast.60), channel_id=1, replica_groups=mesh['cuts'=4,'tile'=8] {'tile'}, dimensions={0} | all-to-all | bytes 1048576 | tf_op jit(solution)/shard_map/all_to_all | solution.py:97
  292.3 0.8 copy.23
  293.1 0.0 copy-done.2
  (15 shorter events, 0.3 us)
Async XLA Ops:
  8.7 62.1 %all-to-all-start = ((s32[8,1,1280]{2,1,0:T(1,128)}), s32[8,1,1280]{2,1,0:T(1,128)S(1)}, u32[]{:S(2)}, u32[]{:S(2)}) async-start(s32[8,1,1280]{2,1,0:T(1,128)} %compare_select_fusion.1), calls=%async_computation | async-start | bytes 81920 | tf_op jit(solution)/shard_map/all_to_all | solution.py:67
  70.7 121.2 %all-to-all-start.1 = ((bf16[8,1280,256]{2,1,0:T(8,128)(2,1)}), bf16[8,1280,256]{2,1,0:T(8,128)(2,1)}, u32[]{:S(2)}, u32[]{:S(2)}) async-start(bf16[8,1280,256]{2,1,0:T(8,128)(2,1)} %select_select_fusion), calls=%async_computation.1 | async-start | bytes 10485760 | tf_op jit(solution)/shard_map/all_to_all | solution.py:66
  76.7 159.3 %reduce-scatter.2.cloned.1.call-start = ((), (), s32[]{:S(2)}) async-start(), calls=%async_computation.4 | async-start | bytes 1310720 | tf_op jit(solution)/shard_map/reduce_scatter | solution.py:77
  191.9 20.0 %copy-start.1 = (bf16[256,1024]{1,0:T(8,128)(2,1)S(1)}, bf16[256,1024]{1,0:T(8,128)(2,1)}, u32[]{:S(2)}) copy-start(bf16[256,1024]{1,0:T(8,128)(2,1)} %param.10) | copy-start | bytes 1572868
  210.9 1.0 copy-start
  210.9 48.8 %copy-start.4 = (s32[1,8]{1,0:T(1,128)S(1)}, s32[1,8]{1,0:T(1,128)}, u32[]{:S(2)}) copy-start(s32[1,8]{1,0:T(1,128)} %param.15) | copy-start | bytes 100
  210.9 59.3 %copy-start.3 = (s32[1,8,128]{2,1,0:T(8,128)S(1)}, s32[1,8,128]{2,1,0:T(8,128)}, u32[]{:S(2)}) copy-start(s32[1,8,128]{2,1,0:T(8,128)} %param.14) | copy-start | bytes 12292
  237.8 9.9 %collective-permute-start = (f32[1,256,256]{2,1,0:T(8,128)S(1)}, f32[1,256,256]{2,1,0:T(8,128)S(1)}, u32[]{:S(2)}, u32[]{:S(2)}) collective-permute-start(f32[1,256,256]{2,1,0:T(8,128)S(1)} %fusion.23), channel_id=1, source_target_pairs={{1,0},{2,1},{3,2},{4,3},{5,4},{6,5},{7,6},{8,7},{9,8},{10,9},{11,1... | collective-permute-start | bytes 786440 | tf_op jit(solution)/shard_map/ppermute | solution.py:23
  239.1 14.1 %collective-permute-start.1 = (f32[1,256,256]{2,1,0:T(8,128)S(1)}, f32[1,256,256]{2,1,0:T(8,128)S(1)}, u32[]{:S(2)}, u32[]{:S(2)}) collective-permute-start(f32[1,256,256]{2,1,0:T(8,128)S(1)} %fusion.23), channel_id=1, source_target_pairs={{0,1},{1,2},{2,3},{3,4},{4,5},{5,6},{6,7},{7,8},{8,9},{9,10},{10,1... | collective-permute-start | bytes 786440 | tf_op jit(solution)/shard_map/ppermute | solution.py:21
  253.3 8.9 %collective-permute-start.2 = (f32[1,256,256]{2,1,0:T(8,128)S(1)}, f32[1,256,256]{2,1,0:T(8,128)S(1)}, u32[]{:S(2)}, u32[]{:S(2)}) collective-permute-start(f32[1,256,256]{2,1,0:T(8,128)S(1)} %fusion.14), channel_id=1, source_target_pairs={{1,0},{2,1},{3,2},{4,3},{5,4},{6,5},{7,6},{8,7},{9,8},{10,9},{11,1... | collective-permute-start | bytes 786440 | tf_op jit(solution)/shard_map/ppermute | solution.py:23
  254.7 15.3 %collective-permute-start.3 = (f32[1,256,256]{2,1,0:T(8,128)S(1)}, f32[1,256,256]{2,1,0:T(8,128)S(1)}, u32[]{:S(2)}, u32[]{:S(2)}) collective-permute-start(f32[1,256,256]{2,1,0:T(8,128)S(1)} %fusion.14), channel_id=1, source_target_pairs={{0,1},{1,2},{2,3},{3,4},{4,5},{5,6},{6,7},{7,8},{8,9},{9,10},{10,1... | collective-permute-start | bytes 786440 | tf_op jit(solution)/shard_map/ppermute | solution.py:21
  270.2 22.9 %copy-start.2 = (bf16[1,256,256]{2,1,0:T(8,128)(2,1)}, bf16[1,256,256]{2,1,0:T(8,128)(2,1)S(1)}, u32[]{:S(2)}) copy-start(bf16[1,256,256]{2,1,0:T(8,128)(2,1)S(1)} %fusion.20) | copy-start | bytes 393220
Sparse Core Ops, SparseCore 0:
  212.0 23.9 reduce-scatter.1
where the time goes:
time: 301 us; the launch traced here: 300 us
  waiting for transfers between devices  159 us (53%)
  local copies, waits for them, and re-layouts  46.1 us (15%)
  starting transfers between devices  25.5 us (8%)
  blocking collectives  21.6 us (7%)
  matrix products  20.5 us (7%)
  between operations  14.2 us (5%)
  other arithmetic  13 us (4%)
    all_to_all x1, waiting for transfers between devices, local(): lax.all_to_all(picked, 'tile', split_axis=0, concat_axis=0, tiled=True)  115 us
    gather x1, local copies, waits for them, and re-layouts, local(): jnp.take(acquired, slots.reshape(-1), axis=0)  43 us
    reduce_scatter x1, waiting for transfers between devices, local(): lax.psum_scatter(line_planes, 'cuts', scatter_dimension=0, tiled=True)  23.9 us
    all_to_all x1, blocking collectives, local(): lax.all_to_all(outgoing, 'tile', split_axis=0, concat_axis=0, tiled=True)  21.6 us
    dot_general x8, matrix products, line_sums(): return jnp.dot(onehot, rows_block, preferred_element_type=jnp.float32)  18.5 us
    ppermute x2, waiting for transfers between devices, with_halo(): lax.ppermute(tail, axis, [(i, (i + 1) % count) for i in range(ends)])  13.2 us
    ppermute x2, starting transfers between devices, with_halo(): lax.ppermute(tail, axis, [(i, (i + 1) % count) for i in range(ends)])  9.59 us
    select_n x1, other arithmetic, local(): picked = jnp.where(usable[:, :, None], picked, jnp.zeros_like(picked))  9.36 us
  transfers between devices with their start and end apart: 7, of which 6 were waited for; matrix products, arithmetic and copies ran while one was open for 18% of the time, Pallas kernels for 0%

commit v1 on v0

--- a/solution.py
+++ b/solution.py
@@ -1,6 +1,10 @@
+import functools
+
 import jax
 import jax.numpy as jnp
 from jax import lax
+from jax.experimental import pallas as pl
+from jax.experimental.pallas import tpu as pltpu
 from jax.sharding import PartitionSpec as P
 
 NX = 256
@@ -8,6 +12,89 @@
 TAPS = 4
 ITERS = 2
 ZDEV = 1
+LOAD_ROWS = 1024
+UNROLL = 8
+
+
+def line_sum_kernel(slots, lines, counts, acquired, out, rows, staged, even, odd, load_sem):
+    tile = pl.program_id(0)
+    loads = acquired.shape[0] // LOAD_ROWS
+
+    def load(step):
+        return pltpu.make_async_copy(
+            acquired.at[pl.ds(pl.multiple_of(step * LOAD_ROWS, LOAD_ROWS), LOAD_ROWS)],
+            staged.at[step],
+            load_sem.at[step],
+        )
+
+    @pl.when(tile == 0)
+    def _():
+        @pl.loop(0, loads)
+        def _(step):
+            load(step).start()
+
+        @pl.loop(0, loads)
+        def _(step):
+            load(step).wait()
+            rows[pl.ds(pl.multiple_of(step * LOAD_ROWS, LOAD_ROWS), LOAD_ROWS), :] = staged[
+                step
+            ].astype(jnp.float32)
+
+    even[...] = jnp.zeros_like(even)
+    odd[...] = jnp.zeros_like(odd)
+    count = counts[0, tile]
+
+    def add(j, total):
+        line = lines[0, tile, j]
+        total[pl.ds(line, 1), :] += rows[pl.ds(slots[0, tile, j], 1), :]
+
+    groups = count // UNROLL
+
+    @pl.loop(0, groups)
+    def _(group):
+        for u in range(UNROLL):
+            add(group * UNROLL + u, (even, odd)[u % 2])
+
+    @pl.loop(groups * UNROLL, count)
+    def _(j):
+        add(j, even)
+
+    cores, others = out.shape[0], out.shape[1]
+    for core in range(cores):
+        for x in range(others):
+            span = pl.ds((x * cores + core) * NY, NY)
+            out[core, x, 0] = even[span, :] + odd[span, :]
+
+
+def line_sums(acquired, slots, lines, counts, cut_count):
+    tile_count = slots.shape[1]
+    cores = 2
+    rows_dev = acquired.shape[0]
+    loads = rows_dev // LOAD_ROWS
+    group_lines = cut_count * NY
+    return pl.pallas_call(
+        line_sum_kernel,
+        grid=(tile_count,),
+        out_shape=jax.ShapeDtypeStruct((cores, cut_count // cores, tile_count, NY, NX), jnp.float32),
+        in_specs=[
+            pl.BlockSpec(memory_space=pltpu.SMEM),
+            pl.BlockSpec(memory_space=pltpu.SMEM),
+            pl.BlockSpec(memory_space=pltpu.SMEM),
+            pl.BlockSpec(memory_space=pl.ANY),
+        ],
+        out_specs=pl.BlockSpec(
+            (cores, cut_count // cores, 1, NY, NX), lambda t: (0, 0, t, 0, 0)
+        ),
+        scratch_shapes=[
+            pltpu.VMEM((rows_dev, NX), jnp.float32),
+            pltpu.VMEM((loads, LOAD_ROWS, NX), jnp.bfloat16),
+            pltpu.VMEM((group_lines, NX), jnp.float32),
+            pltpu.VMEM((group_lines, NX), jnp.float32),
+            pltpu.SemaphoreType.DMA((loads,)),
+        ],
+        compiler_params=pltpu.CompilerParams(vmem_limit_bytes=48 * 1024 * 1024),
+        name="line_sums",
+    )(slots, lines, counts, acquired)
 
 
 def with_halo(cells, sides, width):
@@ -33,12 +120,6 @@
     return padded[2:] + padded[:-2] + ypad[:, 2:] + ypad[:, :-2] + xpad[:, :, 2:] + xpad[:, :, :-2]
 
 
-def line_sums(rows_block, lines_block, line_total):
-    line_range = jnp.arange(line_total, dtype=jnp.int32)
-    onehot = (line_range[:, None] == lines_block[None, :]).astype(jnp.bfloat16)
-    return jnp.dot(onehot, rows_block, preferred_element_type=jnp.float32)
-
-
 def apply_stencil(line_field, stencil):
     plane_total = line_field.shape[0] // NY
     product = jnp.dot(line_field, stencil.astype(jnp.float32), precision=lax.Precision.HIGHEST)
@@ -52,29 +133,9 @@
 def local(acquired, stencil, send_slots, send_lines, send_counts, return_slots, return_counts):
     tile_count = lax.axis_size("tile")
     cut_count = lax.axis_size("cuts")
-    slots = send_slots[0]
-    line_ids = send_lines[0]
-    counts = send_counts[0]
-    slot_total = slots.shape[1]
-    slot_index = jnp.arange(slot_total, dtype=jnp.int32)
-    usable = slot_index[None, :] < counts[:, None]
-    picked = jnp.take(acquired, slots.reshape(-1), axis=0).reshape(tile_count, slot_total, NX)
-    picked = jnp.where(usable[:, :, None], picked, jnp.zeros_like(picked))
-    line_ids = jnp.where(usable, line_ids, 0)
-    group_lines = cut_count * ZDEV * NY
-    arrived, arrived_lines = (
-        lax.all_to_all(picked, "tile", split_axis=0, concat_axis=0, tiled=True),
-        lax.all_to_all(line_ids, "tile", split_axis=0, concat_axis=0, tiled=True),
-    )
-
-    def add_source(carry_lines, source_item):
-        rows_block, lines_block = source_item
-        return (carry_lines + line_sums(rows_block, lines_block, group_lines), None)
-
-    line_buffer = jnp.zeros((group_lines, NX), jnp.float32)
-    line_buffer, _ = lax.scan(add_source, line_buffer, (arrived, arrived_lines))
-    line_planes = line_buffer.reshape(cut_count * ZDEV, NY, NX)
-    own_lines = lax.psum_scatter(line_planes, "cuts", scatter_dimension=0, tiled=True)
+    sums = line_sums(acquired, send_slots, send_lines, send_counts, cut_count)
+    sums = sums.transpose(1, 0, 2, 3, 4).reshape(cut_count * tile_count, NY, NX)
+    own_lines = lax.psum_scatter(sums, ("cuts", "tile"), scatter_dimension=0, tiled=True)
     smooth_field = apply_stencil(own_lines.reshape(ZDEV * NY, NX), stencil)
     for sweep in range(ITERS):
         padded = with_halo(smooth_field, ((("cuts", "tile"), 0),), 1)

time: 301 us -> 300 us (level)
  the two profiles are of different devices: /device:TPU:0 before, /device:TPU:14 now
where the time goes in v1:
time: 300 us; the launch traced here: 295 us
  waiting for transfers between devices  201 us (67%)
  Pallas kernels  33.4 us (11%)
  blocking collectives  18.4 us (6%)
  between operations  14.2 us (5%)
  starting transfers between devices  13.5 us (4%)
  local copies, waits for them, and re-layouts  11.8 us (4%)
    reduce_scatter x1, waiting for transfers between devices, local(): lax.psum_scatter(sums, ('cuts', 'tile'), scatter_dimension=0, tiled=True)  183 us
    pallas_call x1, Pallas kernels, line_sums(): pl.pallas_call(line_sum_kernel, grid=(tile_count,), out_shape=jax.ShapeDt...  33.4 us
    all_to_all x1, blocking collectives, local(): lax.all_to_all(outgoing, 'tile', split_axis=0, concat_axis=0, tiled=True)  18.4 us
    ppermute x2, waiting for transfers between devices, with_halo(): lax.ppermute(head, axis, [((i + 1) % count, i) for i in range(ends)])  11.7 us
    ppermute x2, starting transfers between devices, with_halo(): lax.ppermute(tail, axis, [(i, (i + 1) % count) for i in range(ends)])  9.64 us
    transpose x1, local copies, waits for them, and re-layouts, local(): sums = sums.transpose(1, 0, 2, 3, 4).reshape(cut_count * tile_count, NY, NX)  7.47 us
  transfers between devices with their start and end apart: 5, of which 5 were waited for; matrix products, arithmetic and copies ran while one was open for 0% of the time, Pallas kernels for 0%

profile of v1, /device:TPU:14, one launch (start us, length us, event | category | flops | bytes accessed | tf_op | source)
XLA Modules:
  0.0 294.9 jit_solution(16715184646164597344)
XLA Ops:
  7.2 0.0 reduce-scatter.2.cloned.1.call-start
  7.2 0.0 copy-start
  7.2 0.8 copy-done
  8.0 0.0 copy-start.1
  8.0 0.8 copy-done.1
  8.8 0.0 copy-start.2
  8.8 0.7 copy-done.2
  9.4 33.4 %line_sums.1 = f32[2,2,8,256,256]{4,3,2,1,0:T(8,128)} custom-call(s32[1,8,1280]{2,1,0:T(8,128)S(1)} %copy-done, s32[1,8,1280]{2,1,0:T(8,128)S(1)} %copy-done.1, s32[1,8]{1,0:T(1,128)S(1)} %copy-done.2, bf16[16384,256]{1,0:T(8,128)(2,1)} %acquired.1), custom_call_target="tpu_custom_call" | custom-call | tf_op jit(solution)/shard_map/line_sums/pallas_call | solution.py:75
  42.9 7.5 %copy.10 = f32[2,2,8,256,256]{4,3,2,1,0:T(8,128)} copy(f32[2,2,8,256,256]{4,3,2,0,1:T(8,128)} %bitcast.37) | data formatting | bytes 16777216 | tf_op jit(solution)/shard_map/transpose | solution.py:137
  50.3 0.0 copy-start.3
  50.3 0.0 copy-start.6
  50.3 0.0 copy-start.5
  50.4 0.0 reduce-scatter.2.cloned.1.call-update
  50.4 1.0 copy-done.3
  51.4 0.2 copy.12
  51.6 183.5 %reduce-scatter.2.cloned.1.call-done = f32[1,256,256]{2,1,0:T(8,128)} async-done(((f32[32,256,256]{2,1,0:T(8,128)}), f32[1,256,256]{2,1,0:T(8,128)}) %reduce-scatter.2.cloned.1.call-update) | async-done | bytes 262160 | tf_op jit(solution)/shard_map/reduce_scatter | solution.py:138
  235.1 1.6 convolution_bitcast_fusion
  236.7 0.1 slice_bitcast_fusion
  236.7 0.1 fusion.17
  236.8 1.9 collective-permute-start
  238.8 4.8 %collective-permute-start.1 = (f32[1,256,256]{2,1,0:T(8,128)S(1)}, f32[1,256,256]{2,1,0:T(8,128)S(1)}, u32[]{:S(2)}, u32[]{:S(2)}) collective-permute-start(f32[1,256,256]{2,1,0:T(8,128)S(1)} %fusion.17), channel_id=1, source_target_pairs={{0,1},{1,2},{2,3},{3,4},{4,5},{5,6},{6,7},{7,8},{8,9},{9,10},{10,1... | collective-permute-start | bytes 786440 | tf_op jit(solution)/shard_map/ppermute | solution.py:108
  243.6 5.0 %collective-permute-done = f32[1,256,256]{2,1,0:T(8,128)S(1)} collective-permute-done((f32[1,256,256]{2,1,0:T(8,128)S(1)}, f32[1,256,256]{2,1,0:T(8,128)S(1)}, u32[]{:S(2)}, u32[]{:S(2)}) %collective-permute-start) | collective-permute-done | bytes 262176 | tf_op jit(solution)/shard_map/ppermute | solution.py:110
  248.6 2.8 collective-permute-done.1
  251.5 0.2 fusion.8
  251.7 1.9 collective-permute-start.2
  253.6 4.8 %collective-permute-start.3 = (f32[1,256,256]{2,1,0:T(8,128)S(1)}, f32[1,256,256]{2,1,0:T(8,128)S(1)}, u32[]{:S(2)}, u32[]{:S(2)}) collective-permute-start(f32[1,256,256]{2,1,0:T(8,128)S(1)} %fusion.8), channel_id=1, source_target_pairs={{0,1},{1,2},{2,3},{3,4},{4,5},{5,6},{6,7},{7,8},{8,9},{9,10},{10,1... | collective-permute-start | bytes 786440 | tf_op jit(solution)/shard_map/ppermute | solution.py:108
  258.4 0.0 copy-done.6
  258.4 0.1 fusion.20
  258.5 6.6 %collective-permute-done.2 = f32[1,256,256]{2,1,0:T(8,128)S(1)} collective-permute-done((f32[1,256,256]{2,1,0:T(8,128)S(1)}, f32[1,256,256]{2,1,0:T(8,128)S(1)}, u32[]{:S(2)}, u32[]{:S(2)}) %collective-permute-start.2) | collective-permute-done | bytes 262176 | tf_op jit(solution)/shard_map/ppermute | solution.py:110
  265.1 3.1 %collective-permute-done.3 = f32[1,256,256]{2,1,0:T(8,128)S(1)} collective-permute-done((f32[1,256,256]{2,1,0:T(8,128)S(1)}, f32[1,256,256]{2,1,0:T(8,128)S(1)}, u32[]{:S(2)}, u32[]{:S(2)}) %collective-permute-start.3) | collective-permute-done | bytes 262176 | tf_op jit(solution)/shard_map/ppermute | solution.py:108
  268.2 0.2 fusion.14
  268.4 0.0 copy-start.4
  268.4 0.0 copy-done.5
  268.4 0.5 convolution_convert_fusion
  268.9 18.4 %all_to_all.5 = bf16[8,128,256]{2,1,0:T(8,128)(2,1)S(1)} all-to-all(bf16[8,128,256]{2,1,0:T(8,128)(2,1)S(1)} %bitcast.43), channel_id=1, replica_groups=mesh['cuts'=4,'tile'=8] {'tile'}, dimensions={0} | all-to-all | bytes 1048576 | tf_op jit(solution)/shard_map/all_to_all | solution.py:158
  287.3 0.8 copy.14
  288.1 0.0 copy-done.4
  (3 shorter events, 0.0 us)
Async XLA Ops:
  7.2 227.9 %reduce-scatter.2.cloned.1.call-start = ((), (), s32[]{:S(2)}) async-start(), calls=%async_computation.2 | async-start | bytes 8650752 | tf_op jit(solution)/shard_map/reduce_scatter | solution.py:138
  7.2 0.8 copy-start
  8.0 0.8 copy-start.1
  8.8 0.7 copy-start.2
  50.3 1.0 copy-start.3
  50.3 208.1 %copy-start.6 = (s32[1,8]{1,0:T(1,128)S(1)}, s32[1,8]{1,0:T(1,128)}, u32[]{:S(2)}) copy-start(s32[1,8]{1,0:T(1,128)} %param.13) | copy-start | bytes 100
  50.3 218.1 %copy-start.5 = (s32[1,8,128]{2,1,0:T(8,128)S(1)}, s32[1,8,128]{2,1,0:T(8,128)}, u32[]{:S(2)}) copy-start(s32[1,8,128]{2,1,0:T(8,128)} %param.12) | copy-start | bytes 12292
  236.8 11.8 %collective-permute-start = (f32[1,256,256]{2,1,0:T(8,128)S(1)}, f32[1,256,256]{2,1,0:T(8,128)S(1)}, u32[]{:S(2)}, u32[]{:S(2)}) collective-permute-start(f32[1,256,256]{2,1,0:T(8,128)S(1)} %fusion.17), channel_id=1, source_target_pairs={{1,0},{2,1},{3,2},{4,3},{5,4},{6,5},{7,6},{8,7},{9,8},{10,9},{11,1... | collective-permute-start | bytes 786440 | tf_op jit(solution)/shard_map/ppermute | solution.py:110
  238.8 12.7 %collective-permute-start.1 = (f32[1,256,256]{2,1,0:T(8,128)S(1)}, f32[1,256,256]{2,1,0:T(8,128)S(1)}, u32[]{:S(2)}, u32[]{:S(2)}) collective-permute-start(f32[1,256,256]{2,1,0:T(8,128)S(1)} %fusion.17), channel_id=1, source_target_pairs={{0,1},{1,2},{2,3},{3,4},{4,5},{5,6},{6,7},{7,8},{8,9},{9,10},{10,1... | collective-permute-start | bytes 786440 | tf_op jit(solution)/shard_map/ppermute | solution.py:108
  251.7 13.5 %collective-permute-start.2 = (f32[1,256,256]{2,1,0:T(8,128)S(1)}, f32[1,256,256]{2,1,0:T(8,128)S(1)}, u32[]{:S(2)}, u32[]{:S(2)}) collective-permute-start(f32[1,256,256]{2,1,0:T(8,128)S(1)} %fusion.8), channel_id=1, source_target_pairs={{1,0},{2,1},{3,2},{4,3},{5,4},{6,5},{7,6},{8,7},{9,8},{10,9},{11,1... | collective-permute-start | bytes 786440 | tf_op jit(solution)/shard_map/ppermute | solution.py:110
  253.6 14.6 %collective-permute-start.3 = (f32[1,256,256]{2,1,0:T(8,128)S(1)}, f32[1,256,256]{2,1,0:T(8,128)S(1)}, u32[]{:S(2)}, u32[]{:S(2)}) collective-permute-start(f32[1,256,256]{2,1,0:T(8,128)S(1)} %fusion.8), channel_id=1, source_target_pairs={{0,1},{1,2},{2,3},{3,4},{4,5},{5,6},{6,7},{7,8},{8,9},{9,10},{10,1... | collective-permute-start | bytes 786440 | tf_op jit(solution)/shard_map/ppermute | solution.py:108
  268.4 19.7 %copy-start.4 = (bf16[1,256,256]{2,1,0:T(8,128)(2,1)}, bf16[1,256,256]{2,1,0:T(8,128)(2,1)S(1)}, u32[]{:S(2)}) copy-start(bf16[1,256,256]{2,1,0:T(8,128)(2,1)S(1)} %fusion.14) | copy-start | bytes 393220
Sparse Core Ops, SparseCore 0:
  50.5 184.5 reduce-scatter.1

commit v2 on v1

v2 whole, which is shorter than its diff:
```python
import jax
import jax.numpy as jnp
from jax import lax
from jax.experimental import pallas as pl
from jax.experimental.pallas import tpu as pltpu
from jax.sharding import PartitionSpec as P

NX = 256
NY = 256
TAPS = 4
ZDEV = 1
LOAD_ROWS = 1024
UNROLL = 8
LEVELS = 32767.0
WEIGHT = 0.15


def line_sum_kernel(slots, lines, counts, acquired, out, rows, staged, even, odd, load_sem):
    tile = pl.program_id(0)
    loads = acquired.shape[0] // LOAD_ROWS

    def load(step):
        return pltpu.make_async_copy(
            acquired.at[pl.ds(pl.multiple_of(step * LOAD_ROWS, LOAD_ROWS), LOAD_ROWS)],
            staged.at[step],
            load_sem.at[step],
        )

    @pl.when(tile == 0)
    def _():
        @pl.loop(0, loads)
        def _(step):
            load(step).start()

        @pl.loop(0, loads)
        def _(step):
            load(step).wait()
            rows[pl.ds(pl.multiple_of(step * LOAD_ROWS, LOAD_ROWS), LOAD_ROWS), :] = staged[
                step
            ].astype(jnp.float32)

    even[...] = jnp.zeros_like(even)
    odd[...] = jnp.zeros_like(odd)
    count = counts[0, tile]

    def add(j, total):
        line = lines[0, tile, j]
        total[pl.ds(line, 1), :] += rows[pl.ds(slots[0, tile, j], 1), :]

    groups = count // UNROLL

    @pl.loop(0, groups)
    def _(group):
        for u in range(UNROLL):
            add(group * UNROLL + u, (even, odd)[u % 2])

    @pl.loop(groups * UNROLL, count)
    def _(j):
        add(j, even)

    cores, others = out.shape[0], out.shape[1]
    for core in range(cores):
        for x in range(others):
            span = pl.ds((x * cores + core) * NY, NY)
            out[core, x, 0] = even[span, :] + odd[span, :]


def line_sums(acquired, slots, lines, counts, cut_count):
    tile_count = slots.shape[1]
    cores = 2
    rows_dev = acquired.shape[0]
    loads = rows_dev // LOAD_ROWS
    group_lines = cut_count * NY
    return pl.pallas_call(
        line_sum_kernel,
        grid=(tile_count,),
        out_shape=jax.ShapeDtypeStruct((cores, cut_count // cores, tile_count, NY, NX), jnp.float32),
        in_specs=[
            pl.BlockSpec(memory_space=pltpu.SMEM),
            pl.BlockSpec(memory_space=pltpu.SMEM),
            pl.BlockSpec(memory_space=pltpu.SMEM),
            pl.BlockSpec(memory_space=pl.ANY),
        ],
        out_specs=pl.BlockSpec(
            (cores, cut_count // cores, 1, NY, NX), lambda t: (0, 0, t, 0, 0)
        ),
        scratch_shapes=[
            pltpu.VMEM((rows_dev, NX), jnp.float32),
            pltpu.VMEM((loads, LOAD_ROWS, NX), jnp.bfloat16),
            pltpu.VMEM((group_lines, NX), jnp.float32),
            pltpu.VMEM((group_lines, NX), jnp.float32),
            pltpu.SemaphoreType.DMA((loads,)),
        ],
        compiler_params=pltpu.CompilerParams(vmem_limit_bytes=48 * 1024 * 1024),
        name="line_sums",
    )(slots, lines, counts, acquired)


def code(plane):
    most = jnp.max(jnp.abs(plane), axis=0, keepdims=True)
    most = jnp.maximum(most, 1e-30)
    coded = jnp.round(plane * (LEVELS / most)).astype(jnp.int32).astype(jnp.int16)
    return coded, jnp.broadcast_to(most * (1.0 / LEVELS), (8, NX))


def decode(coded, scale):
    return coded.astype(jnp.int32).astype(jnp.float32) * scale[0:1, :]


def shifted(plane, by, axis):
    zeros = jnp.zeros((abs(by), NX) if axis == 0 else (NY, abs(by)), plane.dtype)
    size = plane.shape[axis]
    if by > 0:
        return jnp.concatenate([zeros, lax.slice_in_dim(plane, 0, size - by, axis=axis)], axis)
    return jnp.concatenate([lax.slice_in_dim(plane, -by, size, axis=axis), zeros], axis)


def in_plane(plane):
    around = shifted(plane, 1, 0) + shifted(plane, -1, 0)
    around += shifted(plane, 1, 1) + shifted(plane, -1, 1)
    return (1.0 - 6.0 * WEIGHT) * plane + WEIGHT * around


def field_kernel(
    partial, stencil, selector, field_out, returned,
    own, core_in, q1_out, q1_in, s1_out, s1_in, q2_out, q2_in, s2_out, s2_in,
    q3_out, q3_in, s3_out, s3_in, q4_out, q4_in, s4_out, s4_in, back_out,
    own_sem, core_send, core_recv, send1, recv1, send2, recv2, send3, recv3,
    send4, recv4, send5, recv5,
):
    tiles = partial.shape[2]
    side = partial.shape[1]
    depth = tiles // side
    half = depth // 2
    spread = half * side
    cut, tile = lax.axis_index("cuts"), lax.axis_index("tile")
    x, core = cut // 2, cut % 2
    z, y = tile // side, tile % side
    me = cut * tiles + tile
    last = 2 * side * tiles - 1

    def at(x_to, y_to, z_to):
        return (x_to * 2 + core, z_to * side + y_to)

    def remote(src, dst, send, recv, device):
        return pltpu.make_async_remote_copy(
            src_ref=src, dst_ref=dst, send_sem=send, recv_sem=recv,
            device_id=device, device_id_type=pl.DeviceIdType.MESH,
        )

    partner = (x * 2 + 1 - core, tile)
    barrier = pltpu.get_barrier_semaphore()

    def greet(device):
        pl.semaphore_signal(
            barrier, inc=1, device_id=device, device_id_type=pl.DeviceIdType.MESH
        )

    greet(partner)
    for r in range(1, side):
        greet(at((x + r) % side, y, z))
    for s in range(1, tiles):
        greet((cut, (tile + s) % tiles))
    reach = (-2, -1, 1, 2)
    there = [(me + step >= 0) & (me + step <= last) for step in reach]
    for step, exists in zip(reach, there):
        @pl.when(exists)
        def _():
            greet(((me + step) // tiles, (me + step) % tiles))
    met = 1 + side - 1 + tiles - 1
    for exists in there:
        met = met + jnp.where(exists, 1, 0)
    pl.semaphore_wait(barrier, met)

    def place(r, group, i):
        o, h = i // half, i % half
        if group == 0:
            return (x + r) % side, h * side + (y + 1 + o) % side
        return (x + 1 + o) % side, (half + h) * side + (y + r) % side

    def core_copy(r, group, i):
        x_to, t_to = place(r, group, i)
        return remote(
            partial.at[1 - core, x_to, t_to], core_in.at[r - 1, group, i],
            core_send.at[r - 1, group, i], core_recv.at[r - 1, group, i], partner,
        )

    def own_copy(r, group, i):
        x_to, t_to = place(r, group, i)
        return pltpu.make_async_copy(
            partial.at[core, x_to, t_to], own.at[r - 1, group, i], own_sem.at[r - 1, group, i]
        )

    @pl.loop(0, side * spread)
    def _(n):
        r, i = n // spread + 1, n % spread
        for group in range(2):
            core_copy(r, group, i).start()
            own_copy(r, group, i).start()

    def pair(q_out, q_in, s_out, s_in, send, recv, at_out, at_in, device):
        return (
            remote(q_out.at[at_out], q_in.at[at_in], send.at[(0, *at_in)], recv.at[(0, *at_in)], device),
            remote(s_out.at[at_out], s_in.at[at_in], send.at[(1, *at_in)], recv.at[(1, *at_in)], device),
        )

    def copies1(r, group, i):
        device = at((x + r) % side, y, z) if group == 0 else at(x, (y + r) % side, z)
        slot = (r - 1, group, i)
        return pair(q1_out, q1_in, s1_out, s1_in, send1, recv1, slot, slot, device)

    def copies2(group, o, h):
        r = o + 1
        device = at(x, (y + r) % side, z) if group == 0 else at((x + r) % side, y, z)
        slot = (group, o, h)
        return pair(q2_out, q2_in, s2_out, s2_in, send2, recv2, slot, slot, device)

    def copies3(s):
        slot = (s - 1,)
        return pair(
            q3_out, q3_in, s3_out, s3_in, send3, recv3, slot, slot, at(x, y, (z + s) % depth)
        )

    def chip_sum(r, group, i):
        core_copy(r, group, i).wait_recv()
        own_copy(r, group, i).wait()
        return own[r - 1, group, i] + core_in[r - 1, group, i]

    @pl.loop(0, (side - 1) * spread)
    def _(n):
        r, i = n // spread + 1, n % spread
        for group in range(2):
            q1_out[r - 1, group, i], s1_out[r - 1, group, i] = code(chip_sum(r, group, i))
            for copy in copies1(r, group, i):
                copy.start()

    def kept(group, i):
        total = chip_sum(side, group, i)
        for r in range(1, side):
            for copy in copies1(r, group, i):
                copy.wait_recv()
            total += decode(q1_in[r - 1, group, i], s1_in[r - 1, group, i])
        return total

    @pl.loop(0, (side - 1) * half)
    def _(i):
        o, h = i // half, i % half
        for group in range(2):
            q2_out[group, o, h], s2_out[group, o, h] = code(kept(group, i))
            for copy in copies2(group, o, h):
                copy.start()

    @pl.loop(0, half)
    def _(h):
        i = (side - 1) * half + h
        for group in range(2):
            own[side - 1, group, i] = kept(group, i)

    def column(z_to):
        group, h = z_to // half, z_to % half
        total = own[side - 1, group, (side - 1) * half + h]
        for o in range(side - 1):
            total += decode(q2_in[group, o, h], s2_in[group, o, h])
        return total

    @pl.loop(0, (side - 1) * half)
    def _(i):
        for group in range(2):
            for copy in copies2(group, i // half, i % half):
                copy.wait_recv()

    @pl.loop(1, depth)
    def _(s):
        q3_out[s - 1], s3_out[s - 1] = code(column((z + s) % depth))
        for copy in copies3(s):
            copy.start()

    lines = column(z)
    for s in range(1, depth):
        for copy in copies3(s):
            copy.wait_recv()
        lines += decode(q3_in[s - 1], s3_in[s - 1])

    weights = stencil[...]
    raw = jnp.zeros((NY, NX), jnp.float32)
    rest = lines
    product = jnp.zeros((NY, TAPS * NX), jnp.float32)
    for _ in range(3):
        part = rest.astype(jnp.bfloat16)
        rest = rest - part.astype(jnp.float32)
        product += jnp.dot(part, weights, preferred_element_type=jnp.float32)
    raw = product[:, :NX]
    for k in range(1, TAPS):
        term = product[:, k * NX : (k + 1) * NX]
        raw += jnp.concatenate([term[NY - k :], term[: NY - k]], axis=0)

    q4_out[...], s4_out[...] = code(raw)

    def copies4(n):
        to = me + reach[n]
        device = (to // tiles, to % tiles)
        return (
            remote(q4_out, q4_in.at[n], send4.at[0, n], recv4.at[0, n], device),
            remote(s4_out, s4_in.at[n], send4.at[1, n], recv4.at[1, n], device),
        )

    for n in range(4):
        @pl.when(there[n])
        def _():
            for copy in copies4(n):
                copy.start()

    for n in range(4):
        from_there = there[3 - n]

        @pl.when(from_there)
        def _():
            for copy in copies4(n):
                copy.wait_recv()

        @pl.when(jnp.logical_not(from_there))
        def _():
            q4_in[n] = jnp.zeros((NY, NX), jnp.int16)
            s4_in[n] = jnp.zeros((8, NX), jnp.float32)

    near = decode(q4_in[1], s4_in[1]) + decode(q4_in[2], s4_in[2])
    far = decode(q4_in[0], s4_in[0]) + decode(q4_in[3], s4_in[3])
    beside = jnp.where(there[1], 1.0, 0.0) + jnp.where(there[2], 1.0, 0.0)
    once = in_plane(raw) + (2.0 * WEIGHT) * near
    smooth = in_plane(once) + (WEIGHT * WEIGHT) * (far + beside * raw)
    field = smooth.astype(jnp.bfloat16)
    field_out[0] = field

    reads = returned.shape[1]

    def back(t2):
        chosen = selector[pl.ds(pl.multiple_of(t2 * reads, reads), reads), :]
        return jnp.dot(chosen, field_out[0], preferred_element_type=jnp.float32).astype(jnp.bfloat16)

    def copy5(s):
        return remote(
            back_out.at[s - 1], returned.at[tile], send5.at[s - 1], recv5.at[s - 1],
            (cut, (tile + s) % tiles),
        )

    @pl.loop(1, tiles)
    def _(s):
        back_out[s - 1] = back((tile + s) % tiles)
        copy5(s).start()

    returned[tile] = back(tile)

    @pl.loop(0, side * spread)
    def _(n):
        for group in range(2):
            core_copy(n // spread + 1, group, n % spread).wait_send()

    @pl.loop(0, (side - 1) * spread)
    def _(n):
        for group in range(2):
            for copy in copies1(n // spread + 1, group, n % spread):
                copy.wait_send()

    @pl.loop(0, (side - 1) * half)
    def _(i):
        for group in range(2):
            for copy in copies2(group, i // half, i % half):
                copy.wait_send()

    @pl.loop(1, depth)
    def _(s):
        for copy in copies3(s):
            copy.wait_send()

    for n in range(4):
        @pl.when(there[n])
        def _():
            for copy in copies4(n):
                copy.wait_send()

    @pl.loop(1, tiles)
    def _(s):
        copy5(s).wait_send()
        source = (tile - s + tiles) % tiles
        remote(
            back_out.at[s - 1], returned.at[source], send5.at[s - 1], recv5.at[s - 1],
            (cut, (tile + s) % tiles),
        ).wait_recv()


def finish(partial, stencil, selector, reads):
    side, tiles = partial.shape[1], partial.shape[2]
    depth = tiles // side
    half = depth // 2
    spread = half * side
    dma = pltpu.SemaphoreType.DMA

    def coded(*lead):
        return [
            pltpu.VMEM((*lead, NY, NX), jnp.int16),
            pltpu.VMEM((*lead, NY, NX), jnp.int16),
            pltpu.VMEM((*lead, 8, NX), jnp.float32),
            pltpu.VMEM((*lead, 8, NX), jnp.float32),
        ]

    vmem = pl.BlockSpec(memory_space=pltpu.VMEM)
    return pl.pallas_call(
        field_kernel,
        out_shape=(
            jax.ShapeDtypeStruct((1, NY, NX), jnp.bfloat16),
            jax.ShapeDtypeStruct((tiles, reads, NX), jnp.bfloat16),
        ),
        in_specs=[pl.BlockSpec(memory_space=pl.ANY), vmem, vmem],
        out_specs=(vmem, vmem),
        scratch_shapes=[
            pltpu.VMEM((side, 2, spread, NY, NX), jnp.float32),
            pltpu.VMEM((side, 2, spread, NY, NX), jnp.float32),
            *coded(side - 1, 2, spread),
            *coded(2, side - 1, half),
            *coded(depth - 1),
            pltpu.VMEM((NY, NX), jnp.int16),
            pltpu.VMEM((4, NY, NX), jnp.int16),
            pltpu.VMEM((8, NX), jnp.float32),
            pltpu.VMEM((4, 8, NX), jnp.float32),
            pltpu.VMEM((tiles - 1, reads, NX), jnp.bfloat16),
            dma((side, 2, spread)),
            dma((side, 2, spread)),
            dma((side, 2, spread)),
            dma((2, side - 1, 2, spread)),
            dma((2, side - 1, 2, spread)),
            dma((2, 2, side - 1, half)),
            dma((2, 2, side - 1, half)),
            dma((2, depth - 1)),
            dma((2, depth - 1)),
            dma((2, 4)),
            dma((2, 4)),
            dma((tiles - 1,)),
            dma((tiles - 1,)),
        ],
        compiler_params=pltpu.CompilerParams(
            collective_id=0, has_side_effects=True, vmem_limit_bytes=60 * 1024 * 1024
        ),
        name="reduce_smooth_return",
    )(partial, stencil, selector)


def local(acquired, stencil, send_slots, send_lines, send_counts, return_slots, return_counts):
    cut_count = lax.axis_size("cuts")
    sums = line_sums(acquired, send_slots, send_lines, send_counts, cut_count)
    read_ids, read_counts = return_slots[0], return_counts[0]
    reads = read_ids.shape[1]
    usable = jnp.arange(reads, dtype=jnp.int32)[None, :] < read_counts[:, None]
    wanted = jnp.where(usable, read_ids, -1).reshape(-1)
    selector = (wanted[:, None] == jnp.arange(ZDEV * NY, dtype=jnp.int32)[None, :]).astype(
        jnp.bfloat16
    )
    return finish(sums, stencil, selector, reads)


def solution(mesh):
    in_specs = (
        P(("cuts", "tile"), None),
        P("tile", None),
        P(("cuts", "tile"), None, None),
        P(("cuts", "tile"), None, None),
        P(("cuts", "tile"), None),
        P(("cuts", "tile"), None, None),
        P(("cuts", "tile"), None),
    )
    out_specs = (P(("cuts", "tile"), None, None), P(("cuts", "tile"), None, None))
    return jax.shard_map(local, mesh=mesh, in_specs=in_specs, out_specs=out_specs, check_vma=False)
```

time: 300 us -> 108 us (0.36); the launches traced: 295 us -> 108 us
  waiting for transfers between devices: 201 us -> 0 us
  Pallas kernels: 33.4 us -> 100 us
  blocking collectives: 18.4 us -> 0 us
  between operations: 14.2 us -> 0.65 us
  starting transfers between devices: 13.5 us -> 0 us
  local copies, waits for them, and re-layouts: 11.8 us -> 5.65 us
    reduce_scatter x1 -> x0, waiting for transfers between devices: 183 us -> none  [local(): lax.psum_scatter(sums, ('cuts', 'tile'), scatter_dimension=0, tiled=True)]
    pallas_call x0 -> x1, Pallas kernels: none -> 71.4 us  [finish(): pl.pallas_call(field_kernel, out_shape=(jax.ShapeDtypeStruct((1, NY, NX),...]
    all_to_all x1 -> x0, blocking collectives: 18.4 us -> none  [local(): lax.all_to_all(outgoing, 'tile', split_axis=0, concat_axis=0, tiled=True)]
    ppermute x4 -> x0, waiting for transfers between devices: 17.5 us -> none  [the longest x2 11.7 us: with_halo(): lax.ppermute(head, axis, [((i + 1) % count, i) for i in range(ends)])]
    ppermute x4 -> x0, starting transfers between devices: 13.5 us -> none  [the longest x2 9.64 us: with_halo(): lax.ppermute(tail, axis, [(i, (i + 1) % count) for i in range(ends)])]
    transpose x1 -> x0, local copies, waits for them, and re-layouts: 7.47 us -> none  [local(): sums = sums.transpose(1, 0, 2, 3, 4).reshape(cut_count * tile_count, NY, NX)]
    pallas_call x1, Pallas kernels: 33.4 us -> 28.5 us  [line_sums(): pl.pallas_call(line_sum_kernel, grid=(tile_count,), out_shape=jax.ShapeDt...]
  transfers between devices with their start and end apart: 5 -> 0, of which waited for: 5 -> 0; matrix products, arithmetic and copies ran while one was open for 0% -> 0% of each run, Pallas kernels for 0% -> 0%
where the time goes in v2:
time: 108 us
  Pallas kernels  100 us (93%)
  local copies, waits for them, and re-layouts  5.65 us (5%)
  other arithmetic  1.76 us (2%)
    pallas_call x1, Pallas kernels, finish(): pl.pallas_call(field_kernel, out_shape=(jax.ShapeDtypeStruct((1, NY, NX),...  71.4 us
    pallas_call x1, Pallas kernels, line_sums(): pl.pallas_call(line_sum_kernel, grid=(tile_count,), out_shape=jax.ShapeDt...  28.5 us
    unnamed x8, local copies, waits for them, and re-layouts  5.65 us

profile of v2, /device:TPU:14, one launch (start us, length us, event | category | flops | bytes accessed | tf_op | source)
XLA Modules:
  0.0 108.0 jit_solution(11132918809948554109)
XLA Ops:
  0.6 0.8 bitcast_select_fusion
  1.4 1.0 fusion.selector
  2.4 0.0 copy-start
  2.4 0.8 copy-done
  3.2 0.0 copy-start.1
  3.2 0.8 copy-done.1
  3.9 0.0 copy-start.2
  3.9 0.7 copy-done.2
  4.6 28.5 %line_sums.1.partial = f32[2,2,8,256,256]{4,3,2,1,0:T(8,128)} custom-call(s32[1,8,1280]{2,1,0:T(8,128)S(1)} %copy-done, s32[1,8,1280]{2,1,0:T(8,128)S(1)} %copy-done.1, s32[1,8]{1,0:T(1,128)S(1)} %copy-done.2, bf16[16384,256]{1,0:T(8,128)(2,1)} %acquired.1), custom_call_target="tpu_custom_call" | custom-call | tf_op jit(solution)/shard_map/line_sums/pallas_call | solution.py:74
  33.2 71.4 %reduce_smooth_return.1 = (bf16[1,256,256]{2,1,0:T(8,128)(2,1)}, bf16[8,128,256]{2,1,0:T(8,128)(2,1)}) custom-call(f32[2,2,8,256,256]{4,3,2,1,0:T(8,128)} %line_sums.1.partial, bf16[256,1024]{1,0:T(8,128)(2,1)} %stencil.1, bf16[1024,256]{1,0:T(8,128)(2,1)} %fusion.selector), custom_call_target="tpu_custom_call" | custom-call | tf_op jit(solution)/shard_map/reduce_smooth_return/pallas_call | solution.py:407
  104.6 1.6 %copy.11 = bf16[1,256,256]{2,1,0:T(8,128)(2,1)} copy(bf16[1,256,256]{2,1,0:T(8,128)(2,1)} %get-tuple-element.4) | data formatting | bytes 262144
  106.2 1.9 %copy.12 = bf16[8,128,256]{2,1,0:T(8,128)(2,1)} copy(bf16[8,128,256]{2,1,0:T(8,128)(2,1)} %get-tuple-element.5) | data formatting | bytes 1048576
Async XLA Ops:
  2.4 0.8 copy-start
  3.2 0.8 copy-start.1
  3.9 0.7 copy-start.2

commit v3 on v2

--- a/solution.py
+++ b/solution.py
@@ -13,9 +13,32 @@
 UNROLL = 8
 LEVELS = 32767.0
 WEIGHT = 0.15
-
-
-def line_sum_kernel(slots, lines, counts, acquired, out, rows, staged, even, odd, load_sem):
+GROUPS = 8
+GROUP = NY // GROUPS
+
+
+def code(plane):
+    coded, scales = [], []
+    for g in range(GROUPS):
+        block = plane[g * GROUP : (g + 1) * GROUP]
+        most = jnp.maximum(jnp.max(jnp.abs(block), axis=0, keepdims=True), 1e-30)
+        coded.append(jnp.round(block * (LEVELS / most)).astype(jnp.int32).astype(jnp.int16))
+        scales.append(most * (1.0 / LEVELS))
+    return jnp.concatenate(coded, axis=0), jnp.concatenate(scales, axis=0)
+
+
+def decode(coded, scale):
+    parts = []
+    for g in range(GROUPS):
+        part = coded[g * GROUP : (g + 1) * GROUP].astype(jnp.int32).astype(jnp.float32)
+        parts.append(part * scale[g : g + 1])
+    return jnp.concatenate(parts, axis=0)
+
+
+def line_sum_kernel(
+    slots_in, lines_in, counts, acquired, kept_out, sent_out, scale_out,
+    rows, staged, even, odd, slots, lines, load_sem, index_sem,
+):
     tile = pl.program_id(0)
     loads = acquired.shape[0] // LOAD_ROWS
 
@@ -26,8 +49,16 @@
             load_sem.at[step],
         )
 
+    index_copies = (
+        pltpu.make_async_copy(slots_in.at[0], slots, index_sem.at[0]),
+        pltpu.make_async_copy(lines_in.at[0], lines, index_sem.at[1]),
+    )
+
     @pl.when(tile == 0)
     def _():
+        for copy in index_copies:
+            copy.start()
+
         @pl.loop(0, loads)
         def _(step):
             load(step).start()
@@ -39,72 +70,73 @@
                 step
             ].astype(jnp.float32)
 
+        for copy in index_copies:
+            copy.wait()
+
     even[...] = jnp.zeros_like(even)
     odd[...] = jnp.zeros_like(odd)
     count = counts[0, tile]
-
-    def add(j, total):
-        line = lines[0, tile, j]
-        total[pl.ds(line, 1), :] += rows[pl.ds(slots[0, tile, j], 1), :]
-
     groups = count // UNROLL
 
     @pl.loop(0, groups)
     def _(group):
-        for u in range(UNROLL):
-            add(group * UNROLL + u, (even, odd)[u % 2])
+        first = group * UNROLL
+        spots = [pl.ds(lines[tile, first + u], 1) for u in range(UNROLL)]
+        added = [rows[pl.ds(slots[tile, first + u], 1), :] for u in range(UNROLL)]
+        for q in range(0, UNROLL, 4):
+            held = [(even, even, odd, odd)[u][spots[q + u], :] for u in range(4)]
+            for p in (0, 2):
+                total = (even, odd)[p // 2]
+                same = jnp.where(spots[q + p].start == spots[q + p + 1].start, 1.0, 0.0)
+                total[spots[q + p], :] = held[p] + added[q + p]
+                total[spots[q + p + 1], :] = held[p + 1] + (added[q + p + 1] + same * added[q + p])
 
     @pl.loop(groups * UNROLL, count)
     def _(j):
-        add(j, even)
-
-    cores, others = out.shape[0], out.shape[1]
-    for core in range(cores):
-        for x in range(others):
-            span = pl.ds((x * cores + core) * NY, NY)
-            out[core, x, 0] = even[span, :] + odd[span, :]
+        even[pl.ds(lines[tile, j], 1), :] += rows[pl.ds(slots[tile, j], 1), :]
+
+    core = lax.axis_index("cuts") % 2
+    for x in range(kept_out.shape[0]):
+        span = pl.ds(pl.multiple_of((x * 2 + core) * NY, NY), NY)
+        kept_out[x, 0] = even[span, :] + odd[span, :]
+        span = pl.ds(pl.multiple_of((x * 2 + 1 - core) * NY, NY), NY)
+        sent_out[x, 0], scale_out[x, 0] = code(even[span, :] + odd[span, :])
 
 
 def line_sums(acquired, slots, lines, counts, cut_count):
     tile_count = slots.shape[1]
-    cores = 2
+    side = cut_count // 2
     rows_dev = acquired.shape[0]
     loads = rows_dev // LOAD_ROWS
     group_lines = cut_count * NY
+    hbm = pl.BlockSpec(memory_space=pl.ANY)
     return pl.pallas_call(
         line_sum_kernel,
         grid=(tile_count,),
-        out_shape=jax.ShapeDtypeStruct((cores, cut_count // cores, tile_count, NY, NX), jnp.float32),
-        in_specs=[
-            pl.BlockSpec(memory_space=pltpu.SMEM),
-            pl.BlockSpec(memory_space=pltpu.SMEM),
-            pl.BlockSpec(memory_space=pltpu.SMEM),
-            pl.BlockSpec(memory_space=pl.ANY),
-        ],
-        out_specs=pl.BlockSpec(
-            (cores, cut_count // cores, 1, NY, NX), lambda t: (0, 0, t, 0, 0)
+        out_shape=(
+            jax.ShapeDtypeStruct((side, tile_count, NY, NX), jnp.float32),
+            jax.ShapeDtypeStruct((side, tile_count, NY, NX), jnp.int16),
+            jax.ShapeDtypeStruct((side, tile_count, GROUPS, NX), jnp.float32),
+        ),
+        in_specs=[hbm, hbm, pl.BlockSpec(memory_space=pltpu.SMEM), hbm],
+        out_specs=(
+            pl.BlockSpec((side, 1, NY, NX), lambda t: (0, t, 0, 0)),
+            pl.BlockSpec((side, 1, NY, NX), lambda t: (0, t, 0, 0)),
+            pl.BlockSpec((side, 1, GROUPS, NX), lambda t: (0, t, 0, 0)),
         ),
         scratch_shapes=[
             pltpu.VMEM((rows_dev, NX), jnp.float32),
             pltpu.VMEM((loads, LOAD_ROWS, NX), jnp.bfloat16),
             pltpu.VMEM((group_lines, NX), jnp.float32),
             pltpu.VMEM((group_lines, NX), jnp.float32),
+            pltpu.SMEM(slots.shape[1:], jnp.int32),
+            pltpu.SMEM(lines.shape[1:], jnp.int32),
             pltpu.SemaphoreType.DMA((loads,)),
+            pltpu.SemaphoreType.DMA((2,)),
         ],
         compiler_params=pltpu.CompilerParams(vmem_limit_bytes=48 * 1024 * 1024),
         name="line_sums",
     )(slots, lines, counts, acquired)
-
-
-def code(plane):
-    most = jnp.max(jnp.abs(plane), axis=0, keepdims=True)
-    most = jnp.maximum(most, 1e-30)
-    coded = jnp.round(plane * (LEVELS / most)).astype(jnp.int32).astype(jnp.int16)
-    return coded, jnp.broadcast_to(most * (1.0 / LEVELS), (8, NX))
-
-
-def decode(coded, scale):
-    return coded.astype(jnp.int32).astype(jnp.float32) * scale[0:1, :]
 
 
 def shifted(plane, by, axis):
@@ -122,14 +154,13 @@
 
 
 def field_kernel(
-    partial, stencil, selector, field_out, returned,
-    own, core_in, q1_out, q1_in, s1_out, s1_in, q2_out, q2_in, s2_out, s2_in,
+    kept_sums, sent_sums, sent_scales, stencil, read_ids, read_counts, field_out, returned,
+    own, core_in, core_scale, chosen, q1_out, q1_in, s1_out, s1_in, q2_out, q2_in, s2_out, s2_in,
     q3_out, q3_in, s3_out, s3_in, q4_out, q4_in, s4_out, s4_in, back_out,
     own_sem, core_send, core_recv, send1, recv1, send2, recv2, send3, recv3,
     send4, recv4, send5, recv5,
 ):
-    tiles = partial.shape[2]
-    side = partial.shape[1]
+    side, tiles = kept_sums.shape[:2]
     depth = tiles // side
     half = depth // 2
     spread = half * side
@@ -173,30 +204,45 @@
     pl.semaphore_wait(barrier, met)
 
     def place(r, group, i):
-        o, h = i // half, i % half
+        h, o = i // side, i % side
         if group == 0:
             return (x + r) % side, h * side + (y + 1 + o) % side
         return (x + 1 + o) % side, (half + h) * side + (y + r) % side
 
-    def core_copy(r, group, i):
+    def core_copies(r, group, i):
         x_to, t_to = place(r, group, i)
-        return remote(
-            partial.at[1 - core, x_to, t_to], core_in.at[r - 1, group, i],
-            core_send.at[r - 1, group, i], core_recv.at[r - 1, group, i], partner,
+        slot = (r - 1, group, i)
+        return (
+            remote(
+                sent_sums.at[x_to, t_to], core_in.at[slot],
+                core_send.at[(0, *slot)], core_recv.at[(0, *slot)], partner,
+            ),
+            remote(
+                sent_scales.at[x_to, t_to], core_scale.at[slot],
+                core_send.at[(1, *slot)], core_recv.at[(1, *slot)], partner,
+            ),
         )
 
     def own_copy(r, group, i):
         x_to, t_to = place(r, group, i)
         return pltpu.make_async_copy(
-            partial.at[core, x_to, t_to], own.at[r - 1, group, i], own_sem.at[r - 1, group, i]
+            kept_sums.at[x_to, t_to], own.at[r - 1, group, i], own_sem.at[r - 1, group, i]
         )
 
     @pl.loop(0, side * spread)
     def _(n):
         r, i = n // spread + 1, n % spread
         for group in range(2):
-            core_copy(r, group, i).start()
+            for copy in core_copies(r, group, i):
+                copy.start()
             own_copy(r, group, i).start()
+
+    reads = returned.shape[1]
+    field_lines = lax.broadcasted_iota(jnp.int32, (NY, reads), 0)
+    read_index = lax.broadcasted_iota(jnp.int32, (1, reads), 1)
+    for t2 in range(tiles):
+        wanted = jnp.where(read_index < read_counts[0, t2], read_ids[0, t2 : t2 + 1, :], -1)
+        chosen[t2] = jnp.where(field_lines == wanted, 1.0, 0.0).astype(jnp.bfloat16)
 
     def pair(q_out, q_in, s_out, s_in, send, recv, at_out, at_in, device):
         return (
@@ -222,9 +268,10 @@
         )
 
     def chip_sum(r, group, i):
-        core_copy(r, group, i).wait_recv()
+        for copy in core_copies(r, group, i):
+            copy.wait_recv()
         own_copy(r, group, i).wait()
-        return own[r - 1, group, i] + core_in[r - 1, group, i]
+        return own[r - 1, group, i] + decode(core_in[r - 1, group, i], core_scale[r - 1, group, i])
 
     @pl.loop(0, (side - 1) * spread)
     def _(n):
@@ -242,38 +289,41 @@
             total += decode(q1_in[r - 1, group, i], s1_in[r - 1, group, i])
         return total
 
-    @pl.loop(0, (side - 1) * half)
-    def _(i):
-        o, h = i // half, i % half
-        for group in range(2):
-            q2_out[group, o, h], s2_out[group, o, h] = code(kept(group, i))
-            for copy in copies2(group, o, h):
-                copy.start()
-
     @pl.loop(0, half)
     def _(h):
-        i = (side - 1) * half + h
-        for group in range(2):
+        for o in range(side - 1):
+            for group in range(2):
+                q2_out[group, o, h], s2_out[group, o, h] = code(kept(group, h * side + o))
+                for copy in copies2(group, o, h):
+                    copy.start()
+        for group in range(2):
+            i = h * side + side - 1
             own[side - 1, group, i] = kept(group, i)
 
     def column(z_to):
         group, h = z_to // half, z_to % half
-        total = own[side - 1, group, (side - 1) * half + h]
+        total = own[side - 1, group, h * side + side - 1]
         for o in range(side - 1):
             total += decode(q2_in[group, o, h], s2_in[group, o, h])
         return total
 
-    @pl.loop(0, (side - 1) * half)
-    def _(i):
-        for group in range(2):
-            for copy in copies2(group, i // half, i % half):
+    def column_of(h, group):
+        for o in range(side - 1):
+            for copy in copies2(group, o, h):
                 copy.wait_recv()
-
-    @pl.loop(1, depth)
-    def _(s):
-        q3_out[s - 1], s3_out[s - 1] = code(column((z + s) % depth))
-        for copy in copies3(s):
-            copy.start()
+        z_to = group * half + h
+        s = (z_to - z + depth) % depth
+
+        @pl.when(s > 0)
+        def _():
+            q3_out[s - 1], s3_out[s - 1] = code(column(z_to))
+            for copy in copies3(s):
+                copy.start()
+
+    @pl.loop(0, half)
+    def _(h):
+        for group in range(2):
+            column_of(h, group)
 
     lines = column(z)
     for s in range(1, depth):
@@ -321,7 +371,7 @@
         @pl.when(jnp.logical_not(from_there))
         def _():
             q4_in[n] = jnp.zeros((NY, NX), jnp.int16)
-            s4_in[n] = jnp.zeros((8, NX), jnp.float32)
+            s4_in[n] = jnp.zeros((GROUPS, NX), jnp.float32)
 
     near = decode(q4_in[1], s4_in[1]) + decode(q4_in[2], s4_in[2])
     far = decode(q4_in[0], s4_in[0]) + decode(q4_in[3], s4_in[3])
@@ -331,11 +381,10 @@
     field = smooth.astype(jnp.bfloat16)
     field_out[0] = field
 
-    reads = returned.shape[1]
-
     def back(t2):
-        chosen = selector[pl.ds(pl.multiple_of(t2 * reads, reads), reads), :]
-        return jnp.dot(chosen, field_out[0], preferred_element_type=jnp.float32).astype(jnp.bfloat16)
+        return lax.dot_general(
+            chosen[t2], field_out[0], (((0,), (0,)), ((), ())), preferred_element_type=jnp.float32
+        ).astype(jnp.bfloat16)
 
     def copy5(s):
         return remote(
@@ -353,7 +402,8 @@
     @pl.loop(0, side * spread)
     def _(n):
         for group in range(2):
-            core_copy(n // spread + 1, group, n % spread).wait_send()
+            for copy in core_copies(n // spread + 1, group, n % spread):
+                copy.wait_send()
 
     @pl.loop(0, (side - 1) * spread)
     def _(n):
@@ -388,8 +438,9 @@
         ).wait_recv()
 
 
-def finish(partial, stencil, selector, reads):
-    side, tiles = partial.shape[1], partial.shape[2]
+def finish(sums, stencil, read_ids, read_counts):
+    side, tiles = sums[0].shape[:2]
+    reads = read_ids.shape[2]
     depth = tiles // side
     half = depth // 2
     spread = half * side
@@ -399,33 +450,36 @@
         return [
             pltpu.VMEM((*lead, NY, NX), jnp.int16),
             pltpu.VMEM((*lead, NY, NX), jnp.int16),
-            pltpu.VMEM((*lead, 8, NX), jnp.float32),
-            pltpu.VMEM((*lead, 8, NX), jnp.float32),
+            pltpu.VMEM((*lead, GROUPS, NX), jnp.float32),
+            pltpu.VMEM((*lead, GROUPS, NX), jnp.float32),
         ]
 
     vmem = pl.BlockSpec(memory_space=pltpu.VMEM)
+    hbm = pl.BlockSpec(memory_space=pl.ANY)
     return pl.pallas_call(
         field_kernel,
         out_shape=(
             jax.ShapeDtypeStruct((1, NY, NX), jnp.bfloat16),
             jax.ShapeDtypeStruct((tiles, reads, NX), jnp.bfloat16),
         ),
-        in_specs=[pl.BlockSpec(memory_space=pl.ANY), vmem, vmem],
+        in_specs=[hbm, hbm, hbm, vmem, vmem, pl.BlockSpec(memory_space=pltpu.SMEM)],
         out_specs=(vmem, vmem),
         scratch_shapes=[
             pltpu.VMEM((side, 2, spread, NY, NX), jnp.float32),
-            pltpu.VMEM((side, 2, spread, NY, NX), jnp.float32),
+            pltpu.VMEM((side, 2, spread, NY, NX), jnp.int16),
+            pltpu.VMEM((side, 2, spread, GROUPS, NX), jnp.float32),
+            pltpu.VMEM((tiles, NY, reads), jnp.bfloat16),
             *coded(side - 1, 2, spread),
             *coded(2, side - 1, half),
             *coded(depth - 1),
             pltpu.VMEM((NY, NX), jnp.int16),
             pltpu.VMEM((4, NY, NX), jnp.int16),
-            pltpu.VMEM((8, NX), jnp.float32),
-            pltpu.VMEM((4, 8, NX), jnp.float32),
+            pltpu.VMEM((GROUPS, NX), jnp.float32),
+            pltpu.VMEM((4, GROUPS, NX), jnp.float32),
             pltpu.VMEM((tiles - 1, reads, NX), jnp.bfloat16),
             dma((side, 2, spread)),
-            dma((side, 2, spread)),
-            dma((side, 2, spread)),
+            dma((2, side, 2, spread)),
+            dma((2, side, 2, spread)),
             dma((2, side - 1, 2, spread)),
             dma((2, side - 1, 2, spread)),
             dma((2, 2, side - 1, half)),
@@ -441,20 +495,13 @@
             collective_id=0, has_side_effects=True, vmem_limit_bytes=60 * 1024 * 1024
         ),
         name="reduce_smooth_return",
-    )(partial, stencil, selector)
+    )(*sums, stencil, read_ids, read_counts)
 
 
 def local(acquired, stencil, send_slots, send_lines, send_counts, return_slots, return_counts):
     cut_count = lax.axis_size("cuts")
     sums = line_sums(acquired, send_slots, send_lines, send_counts, cut_count)
-    read_ids, read_counts = return_slots[0], return_counts[0]
-    reads = read_ids.shape[1]
-    usable = jnp.arange(reads, dtype=jnp.int32)[None, :] < read_counts[:, None]
-    wanted = jnp.where(usable, read_ids, -1).reshape(-1)
-    selector = (wanted[:, None] == jnp.arange(ZDEV * NY, dtype=jnp.int32)[None, :]).astype(
-        jnp.bfloat16
-    )
-    return finish(sums, stencil, selector, reads)
+    return finish(sums, stencil, return_slots, return_counts)
 
 
 def solution(mesh):

time: 108 us -> 112 us (1.037); the launches traced: 108 us -> 110 us
  Pallas kernels: 100 us -> 102 us
  local copies, waits for them, and re-layouts: 5.65 us -> 7.6 us
  other arithmetic: 1.76 us -> 0 us
    pallas_call x1, Pallas kernels: 28.5 us -> 33.3 us  [line_sums(): pl.pallas_call(line_sum_kernel, grid=(tile_count,), out_shape=(jax.ShapeD...]
    pallas_call x1, Pallas kernels: 71.4 us -> 68.9 us  [finish(): pl.pallas_call(field_kernel, out_shape=(jax.ShapeDtypeStruct((1, NY, NX),...]
    unnamed x8 -> x12, local copies, waits for them, and re-layouts: 5.65 us -> 7.6 us
where the time goes in v3:
time: 112 us; the launch traced here: 110 us
  Pallas kernels  102 us (91%)
  local copies, waits for them, and re-layouts  7.6 us (7%)
    pallas_call x1, Pallas kernels, finish(): pl.pallas_call(field_kernel, out_shape=(jax.ShapeDtypeStruct((1, NY, NX),...  68.9 us
    pallas_call x1, Pallas kernels, line_sums(): pl.pallas_call(line_sum_kernel, grid=(tile_count,), out_shape=(jax.ShapeD...  33.3 us
    unnamed x12, local copies, waits for them, and re-layouts  7.6 us

profile of v3, /device:TPU:14, one launch (start us, length us, event | category | flops | bytes accessed | tf_op | source)
XLA Modules:
  0.0 110.5 jit_solution(13130108334136543797)
XLA Ops:
  0.6 0.0 copy-start.2
  0.6 0.8 copy-done.2
  1.4 0.0 copy-start.3
  1.4 0.8 copy-done.3
  2.2 0.0 copy-start.4
  2.2 0.7 copy-done.4
  2.8 33.3 %line_sums.1 = (f32[2,8,256,256]{3,2,1,0:T(8,128)}, s16[2,8,256,256]{3,2,1,0:T(8,128)(2,1)S(1)}, f32[2,8,8,256]{3,2,1,0:T(8,128)S(1)}) custom-call(s32[1,8,1280]{2,1,0:T(8,128)S(1)} %copy-done.2, s32[1,8,1280]{2,1,0:T(8,128)S(1)} %copy-done.3, s32[1,8]{1,0:T(1,128)S(1)} %copy-done.4, bf16[16384,256]{1,0:T(8,128)(2,1)} %acquired.1), custom_call_target="tpu_custom_call" | custom-call | tf_op jit(solution)/shard_map/line_sums/pallas_call | solution.py:113
  36.2 0.0 copy-start
  36.2 1.3 %copy-done = s16[2,8,256,256]{3,2,1,0:T(8,128)(2,1)} copy-done((s16[2,8,256,256]{3,2,1,0:T(8,128)(2,1)}, s16[2,8,256,256]{3,2,1,0:T(8,128)(2,1)S(1)}, u32[]{:S(2)}) %copy-start) | copy-done | bytes 2097176
  37.5 0.0 copy-start.1
  37.5 0.7 copy-done.1
  38.2 68.9 %reduce_smooth_return.1 = (bf16[1,256,256]{2,1,0:T(8,128)(2,1)}, bf16[8,128,256]{2,1,0:T(8,128)(2,1)}) custom-call(f32[2,8,256,256]{3,2,1,0:T(8,128)} %get-tuple-element.5.kept_sums, s16[2,8,256,256]{3,2,1,0:T(8,128)(2,1)} %copy-done, f32[2,8,8,256]{3,2,1,0:T(8,128)} %copy-done.1, bf16[256,1024]{1,0:T(8,128)(2,1)} %stencil.1, s32[1,8,128]{2,1,0:T(8,128)} %read_ids.1, ...), custom_call_target="tpu_custom_call" | custom-call | tf_op jit(solution)/shard_map/reduce_smooth_return/pallas_call | solution.py:459
  107.0 1.6 %copy.11 = bf16[1,256,256]{2,1,0:T(8,128)(2,1)} copy(bf16[1,256,256]{2,1,0:T(8,128)(2,1)} %get-tuple-element.10) | data formatting | bytes 262144
  108.6 1.9 %copy.12 = bf16[8,128,256]{2,1,0:T(8,128)(2,1)} copy(bf16[8,128,256]{2,1,0:T(8,128)(2,1)} %get-tuple-element.11) | data formatting | bytes 1048576
Async XLA Ops:
  0.6 0.8 copy-start.2
  1.4 0.8 copy-start.3
  2.2 0.7 copy-start.4
  36.2 1.3 %copy-start = (s16[2,8,256,256]{3,2,1,0:T(8,128)(2,1)}, s16[2,8,256,256]{3,2,1,0:T(8,128)(2,1)S(1)}, u32[]{:S(2)}) copy-start(s16[2,8,256,256]{3,2,1,0:T(8,128)(2,1)S(1)} %get-tuple-element.6.sent_sums) | copy-start | bytes 6291460
  37.5 0.7 copy-start.1

commit v4 on v3

--- a/solution.py
+++ b/solution.py
@@ -12,9 +12,12 @@
 LOAD_ROWS = 1024
 UNROLL = 8
 LEVELS = 32767.0
+ROUNDER = 12582912.0
 WEIGHT = 0.15
 GROUPS = 8
 GROUP = NY // GROUPS
+LANES = 128
+PARTS = NX // LANES
 
 
 def code(plane):
@@ -22,7 +25,7 @@
     for g in range(GROUPS):
         block = plane[g * GROUP : (g + 1) * GROUP]
         most = jnp.maximum(jnp.max(jnp.abs(block), axis=0, keepdims=True), 1e-30)
-        coded.append(jnp.round(block * (LEVELS / most)).astype(jnp.int32).astype(jnp.int16))
+        coded.append((block * (LEVELS / most) + ROUNDER - ROUNDER).astype(jnp.int32).astype(jnp.int16))
         scales.append(most * (1.0 / LEVELS))
     return jnp.concatenate(coded, axis=0), jnp.concatenate(scales, axis=0)
 
@@ -36,7 +39,7 @@
 
 
 def line_sum_kernel(
-    slots_in, lines_in, counts, acquired, kept_out, sent_out, scale_out,
+    slots_in, lines_in, counts, acquired, kept_out, sent_out,
     rows, staged, even, odd, slots, lines, load_sem, index_sem,
 ):
     tile = pl.program_id(0)
@@ -66,9 +69,12 @@
         @pl.loop(0, loads)
         def _(step):
             load(step).wait()
-            rows[pl.ds(pl.multiple_of(step * LOAD_ROWS, LOAD_ROWS), LOAD_ROWS), :] = staged[
-                step
-            ].astype(jnp.float32)
+            block = staged[step].astype(jnp.float32)
+            first = step * LOAD_ROWS * PARTS
+            for part in range(PARTS):
+                rows[pl.ds(first + part, LOAD_ROWS, stride=PARTS), :] = block[
+                    :, part * LANES : (part + 1) * LANES
+                ]
 
         for copy in index_copies:
             copy.wait()
@@ -78,29 +84,29 @@
     count = counts[0, tile]
     groups = count // UNROLL
 
+    def spot(ref, j):
+        return pl.ds(pl.multiple_of(ref[tile, j] * PARTS, PARTS), PARTS)
+
     @pl.loop(0, groups)
     def _(group):
         first = group * UNROLL
-        spots = [pl.ds(lines[tile, first + u], 1) for u in range(UNROLL)]
-        added = [rows[pl.ds(slots[tile, first + u], 1), :] for u in range(UNROLL)]
-        for q in range(0, UNROLL, 4):
-            held = [(even, even, odd, odd)[u][spots[q + u], :] for u in range(4)]
-            for p in (0, 2):
-                total = (even, odd)[p // 2]
-                same = jnp.where(spots[q + p].start == spots[q + p + 1].start, 1.0, 0.0)
-                total[spots[q + p], :] = held[p] + added[q + p]
-                total[spots[q + p + 1], :] = held[p + 1] + (added[q + p + 1] + same * added[q + p])
+        spots = [spot(lines, first + u) for u in range(UNROLL)]
+        added = [rows[spot(slots, first + u), :] for u in range(UNROLL)]
+        for u in range(UNROLL):
+            total = (even, odd)[u % 2]
+            total[spots[u], :] += added[u]
 
     @pl.loop(groups * UNROLL, count)
     def _(j):
-        even[pl.ds(lines[tile, j], 1), :] += rows[pl.ds(slots[tile, j], 1), :]
+        even[spot(lines, j), :] += rows[spot(slots, j), :]
 
     core = lax.axis_index("cuts") % 2
     for x in range(kept_out.shape[0]):
-        span = pl.ds(pl.multiple_of((x * 2 + core) * NY, NY), NY)
-        kept_out[x, 0] = even[span, :] + odd[span, :]
-        span = pl.ds(pl.multiple_of((x * 2 + 1 - core) * NY, NY), NY)
-        sent_out[x, 0], scale_out[x, 0] = code(even[span, :] + odd[span, :])
+        for out, core_to in ((kept_out, core), (sent_out, 1 - core)):
+            first = (x * 2 + core_to) * NY * PARTS
+            for part in range(PARTS):
+                span = pl.ds(first + part, NY, stride=PARTS)
+                out[x, 0, :, part * LANES : (part + 1) * LANES] = even[span, :] + odd[span, :]
 
 
 def line_sums(acquired, slots, lines, counts, cut_count):
@@ -115,26 +121,24 @@
         grid=(tile_count,),
         out_shape=(
             jax.ShapeDtypeStruct((side, tile_count, NY, NX), jnp.float32),
-            jax.ShapeDtypeStruct((side, tile_count, NY, NX), jnp.int16),
-            jax.ShapeDtypeStruct((side, tile_count, GROUPS, NX), jnp.float32),
+            jax.ShapeDtypeStruct((side, tile_count, NY, NX), jnp.float32),
         ),
         in_specs=[hbm, hbm, pl.BlockSpec(memory_space=pltpu.SMEM), hbm],
         out_specs=(
             pl.BlockSpec((side, 1, NY, NX), lambda t: (0, t, 0, 0)),
             pl.BlockSpec((side, 1, NY, NX), lambda t: (0, t, 0, 0)),
-            pl.BlockSpec((side, 1, GROUPS, NX), lambda t: (0, t, 0, 0)),
         ),
         scratch_shapes=[
-            pltpu.VMEM((rows_dev, NX), jnp.float32),
+            pltpu.VMEM((rows_dev * PARTS, LANES), jnp.float32),
             pltpu.VMEM((loads, LOAD_ROWS, NX), jnp.bfloat16),
-            pltpu.VMEM((group_lines, NX), jnp.float32),
-            pltpu.VMEM((group_lines, NX), jnp.float32),
+            pltpu.VMEM((group_lines * PARTS, LANES), jnp.float32),
+            pltpu.VMEM((group_lines * PARTS, LANES), jnp.float32),
             pltpu.SMEM(slots.shape[1:], jnp.int32),
             pltpu.SMEM(lines.shape[1:], jnp.int32),
             pltpu.SemaphoreType.DMA((loads,)),
             pltpu.SemaphoreType.DMA((2,)),
         ],
-        compiler_params=pltpu.CompilerParams(vmem_limit_bytes=48 * 1024 * 1024),
+        compiler_params=pltpu.CompilerParams(vmem_limit_bytes=62 * 1024 * 1024),
         name="line_sums",
     )(slots, lines, counts, acquired)
 
@@ -154,8 +158,8 @@
 
 
 def field_kernel(
-    kept_sums, sent_sums, sent_scales, stencil, read_ids, read_counts, field_out, returned,
-    own, core_in, core_scale, chosen, q1_out, q1_in, s1_out, s1_in, q2_out, q2_in, s2_out, s2_in,
+    kept_sums, sent_sums, stencil, read_ids, read_counts, field_out, returned,
+    own, core_in, chosen, q1_out, q1_in, s1_out, s1_in, q2_out, q2_in, s2_out, s2_in,
     q3_out, q3_in, s3_out, s3_in, q4_out, q4_in, s4_out, s4_in, back_out,
     own_sem, core_send, core_recv, send1, recv1, send2, recv2, send3, recv3,
     send4, recv4, send5, recv5,
@@ -209,18 +213,11 @@
             return (x + r) % side, h * side + (y + 1 + o) % side
         return (x + 1 + o) % side, (half + h) * side + (y + r) % side
 
-    def core_copies(r, group, i):
+    def core_copy(r, group, i):
         x_to, t_to = place(r, group, i)
         slot = (r - 1, group, i)
-        return (
-            remote(
-                sent_sums.at[x_to, t_to], core_in.at[slot],
-                core_send.at[(0, *slot)], core_recv.at[(0, *slot)], partner,
-            ),
-            remote(
-                sent_scales.at[x_to, t_to], core_scale.at[slot],
-                core_send.at[(1, *slot)], core_recv.at[(1, *slot)], partner,
-            ),
+        return remote(
+            sent_sums.at[x_to, t_to], core_in.at[slot], core_send.at[slot], core_recv.at[slot], partner
         )
 
     def own_copy(r, group, i):
@@ -233,8 +230,7 @@
     def _(n):
         r, i = n // spread + 1, n % spread
         for group in range(2):
-            for copy in core_copies(r, group, i):
-                copy.start()
+            core_copy(r, group, i).start()
             own_copy(r, group, i).start()
 
     reads = returned.shape[1]
@@ -268,10 +264,9 @@
         )
 
     def chip_sum(r, group, i):
-        for copy in core_copies(r, group, i):
-            copy.wait_recv()
+        core_copy(r, group, i).wait_recv()
         own_copy(r, group, i).wait()
-        return own[r - 1, group, i] + decode(core_in[r - 1, group, i], core_scale[r - 1, group, i])
+        return own[r - 1, group, i] + core_in[r - 1, group, i]
 
     @pl.loop(0, (side - 1) * spread)
     def _(n):
@@ -402,8 +397,7 @@
     @pl.loop(0, side * spread)
     def _(n):
         for group in range(2):
-            for copy in core_copies(n // spread + 1, group, n % spread):
-                copy.wait_send()
+            core_copy(n // spread + 1, group, n % spread).wait_send()
 
     @pl.loop(0, (side - 1) * spread)
     def _(n):
@@ -462,12 +456,11 @@
             jax.ShapeDtypeStruct((1, NY, NX), jnp.bfloat16),
             jax.ShapeDtypeStruct((tiles, reads, NX), jnp.bfloat16),
         ),
-        in_specs=[hbm, hbm, hbm, vmem, vmem, pl.BlockSpec(memory_space=pltpu.SMEM)],
+        in_specs=[hbm, hbm, vmem, vmem, pl.BlockSpec(memory_space=pltpu.SMEM)],
         out_specs=(vmem, vmem),
         scratch_shapes=[
             pltpu.VMEM((side, 2, spread, NY, NX), jnp.float32),
-            pltpu.VMEM((side, 2, spread, NY, NX), jnp.int16),
-            pltpu.VMEM((side, 2, spread, GROUPS, NX), jnp.float32),
+            pltpu.VMEM((side, 2, spread, NY, NX), jnp.float32),
             pltpu.VMEM((tiles, NY, reads), jnp.bfloat16),
             *coded(side - 1, 2, spread),
             *coded(2, side - 1, half),
@@ -478,8 +471,8 @@
             pltpu.VMEM((4, GROUPS, NX), jnp.float32),
             pltpu.VMEM((tiles - 1, reads, NX), jnp.bfloat16),
             dma((side, 2, spread)),
-            dma((2, side, 2, spread)),
-            dma((2, side, 2, spread)),
+            dma((side, 2, spread)),
+            dma((side, 2, spread)),
             dma((2, side - 1, 2, spread)),
             dma((2, side - 1, 2, spread)),
             dma((2, 2, side - 1, half)),
@@ -492,7 +485,7 @@
             dma((tiles - 1,)),
         ],
         compiler_params=pltpu.CompilerParams(
-            collective_id=0, has_side_effects=True, vmem_limit_bytes=60 * 1024 * 1024
+            collective_id=0, has_side_effects=True, vmem_limit_bytes=62 * 1024 * 1024
         ),
         name="reduce_smooth_return",
     )(*sums, stencil, read_ids, read_counts)

time: 112 us -> 95.7 us (0.85)
  Pallas kernels: 102 us -> 89.7 us
  local copies, waits for them, and re-layouts: 7.6 us -> 3.44 us
    pallas_call x1, Pallas kernels: 68.9 us -> 61.8 us  [finish(): pl.pallas_call(field_kernel, out_shape=(jax.ShapeDtypeStruct((1, NY, NX),...]
    pallas_call x1, Pallas kernels: 33.3 us -> 27.9 us  [line_sums(): pl.pallas_call(line_sum_kernel, grid=(tile_count,), out_shape=(jax.ShapeD...]
    unnamed x12 -> x2, local copies, waits for them, and re-layouts: 7.6 us -> 3.44 us
where the time goes in v4:
time: 95.7 us; the launch traced here: 93.8 us
  Pallas kernels  89.7 us (94%)
  local copies, waits for them, and re-layouts  3.44 us (4%)
    pallas_call x1, Pallas kernels, finish(): pl.pallas_call(field_kernel, out_shape=(jax.ShapeDtypeStruct((1, NY, NX),...  61.8 us
    pallas_call x1, Pallas kernels, line_sums(): pl.pallas_call(line_sum_kernel, grid=(tile_count,), out_shape=(jax.ShapeD...  27.9 us
    unnamed x2, local copies, waits for them, and re-layouts  3.44 us

profile of v4, /device:TPU:14, one launch (start us, length us, event | category | flops | bytes accessed | tf_op | source)
XLA Modules:
  0.0 93.8 jit_solution(11990979357783705620)
XLA Ops:
  0.6 27.9 %line_sums.1 = (f32[2,8,256,256]{3,2,1,0:T(8,128)}, f32[2,8,256,256]{3,2,1,0:T(8,128)}) custom-call(s32[1,8,1280]{2,1,0:T(8,128)} %slots_in.1, s32[1,8,1280]{2,1,0:T(8,128)} %lines_in.1, s32[1,8]{1,0:T(1,128)} %counts.1, bf16[16384,256]{1,0:T(8,128)(2,1)} %acquired.1), custom_call_target="tpu_custom_call" | custom-call | tf_op jit(solution)/shard_map/line_sums/pallas_call | solution.py:119
  28.6 61.8 %reduce_smooth_return.1 = (bf16[1,256,256]{2,1,0:T(8,128)(2,1)}, bf16[8,128,256]{2,1,0:T(8,128)(2,1)}) custom-call(f32[2,8,256,256]{3,2,1,0:T(8,128)} %get-tuple-element.4.kept_sums, f32[2,8,256,256]{3,2,1,0:T(8,128)} %get-tuple-element.5.sent_sums, bf16[256,1024]{1,0:T(8,128)(2,1)} %stencil.1, s32[1,8,128]{2,1,0:T(8,128)} %read_ids.1, s32[1,8]{1,0:T(1,128)} %read_counts.1), custom_call_target="tpu_custom_call" | custom-call | tf_op jit(solution)/shard_map/reduce_smooth_return/pallas_call | solution.py:453
  90.4 1.6 %copy.11 = bf16[1,256,256]{2,1,0:T(8,128)(2,1)} copy(bf16[1,256,256]{2,1,0:T(8,128)(2,1)} %get-tuple-element.8) | data formatting | bytes 262144
  91.9 1.9 %copy.12 = bf16[8,128,256]{2,1,0:T(8,128)(2,1)} copy(bf16[8,128,256]{2,1,0:T(8,128)(2,1)} %get-tuple-element.9) | data formatting | bytes 1048576

commit v5 on v4

--- a/solution.py
+++ b/solution.py
@@ -92,9 +92,11 @@
         first = group * UNROLL
         spots = [spot(lines, first + u) for u in range(UNROLL)]
         added = [rows[spot(slots, first + u), :] for u in range(UNROLL)]
-        for u in range(UNROLL):
-            total = (even, odd)[u % 2]
-            total[spots[u], :] += added[u]
+        for u in range(0, UNROLL, 2):
+            first_sum = even[spots[u], :] + added[u]
+            second_sum = odd[spots[u + 1], :] + added[u + 1]
+            even[spots[u], :] = first_sum
+            odd[spots[u + 1], :] = second_sum
 
     @pl.loop(groups * UNROLL, count)
     def _(j):
@@ -226,12 +228,15 @@
             kept_sums.at[x_to, t_to], own.at[r - 1, group, i], own_sem.at[r - 1, group, i]
         )
 
-    @pl.loop(0, side * spread)
-    def _(n):
+    def fetch(n):
         r, i = n // spread + 1, n % spread
         for group in range(2):
             core_copy(r, group, i).start()
             own_copy(r, group, i).start()
+
+    @pl.loop(0, (side - 1) * spread)
+    def _(n):
+        fetch(n)
 
     reads = returned.shape[1]
     field_lines = lax.broadcasted_iota(jnp.int32, (NY, reads), 0)
@@ -268,24 +273,35 @@
         own_copy(r, group, i).wait()
         return own[r - 1, group, i] + core_in[r - 1, group, i]
 
-    @pl.loop(0, (side - 1) * spread)
-    def _(n):
-        r, i = n // spread + 1, n % spread
-        for group in range(2):
-            q1_out[r - 1, group, i], s1_out[r - 1, group, i] = code(chip_sum(r, group, i))
-            for copy in copies1(r, group, i):
-                copy.start()
+    def each1(h, act):
+        @pl.loop(0, (side - 1) * side)
+        def _(n):
+            r, i = n // side + 1, h * side + n % side
+            for group in range(2):
+                act(r, group, i)
+
+    def code1(r, group, i):
+        q1_out[r - 1, group, i], s1_out[r - 1, group, i] = code(chip_sum(r, group, i))
+
+    def start1(r, group, i):
+        for copy in copies1(r, group, i):
+            copy.start()
+
+    def arrive1(r, group, i):
+        for copy in copies1(r, group, i):
+            copy.wait_recv()
+
+    def code_start1(r, group, i):
+        code1(r, group, i)
+        start1(r, group, i)
 
     def kept(group, i):
         total = chip_sum(side, group, i)
         for r in range(1, side):
-            for copy in copies1(r, group, i):
-                copy.wait_recv()
             total += decode(q1_in[r - 1, group, i], s1_in[r - 1, group, i])
         return total
 
-    @pl.loop(0, half)
-    def _(h):
+    def step2(h):
         for o in range(side - 1):
             for group in range(2):
                 q2_out[group, o, h], s2_out[group, o, h] = code(kept(group, h * side + o))
@@ -315,8 +331,19 @@
             for copy in copies3(s):
                 copy.start()
 
-    @pl.loop(0, half)
-    def _(h):
+    each1(0, code_start1)
+
+    @pl.loop((side - 1) * spread, side * spread)
+    def _(n):
+        fetch(n)
+
+    for h in range(half):
+        if h + 1 < half:
+            each1(h + 1, code1)
+        each1(h, arrive1)
+        if h + 1 < half:
+            each1(h + 1, start1)
+        step2(h)
         for group in range(2):
             column_of(h, group)
 

time: 95.7 us -> 97.7 us (1.021); the launches traced: 93.8 us -> 97.3 us
  Pallas kernels: 89.7 us -> 93.3 us
    pallas_call x1, Pallas kernels: 61.8 us -> 70.8 us  [finish(): pl.pallas_call(field_kernel, out_shape=(jax.ShapeDtypeStruct((1, NY, NX),...]
    pallas_call x1, Pallas kernels: 27.9 us -> 22.5 us  [line_sums(): pl.pallas_call(line_sum_kernel, grid=(tile_count,), out_shape=(jax.ShapeD...]
where the time goes in v5:
time: 97.7 us; the launch traced here: 97.3 us
  Pallas kernels  93.3 us (95%)
  local copies, waits for them, and re-layouts  3.44 us (4%)
    pallas_call x1, Pallas kernels, finish(): pl.pallas_call(field_kernel, out_shape=(jax.ShapeDtypeStruct((1, NY, NX),...  70.8 us
    pallas_call x1, Pallas kernels, line_sums(): pl.pallas_call(line_sum_kernel, grid=(tile_count,), out_shape=(jax.ShapeD...  22.5 us
    unnamed x2, local copies, waits for them, and re-layouts  3.44 us

profile of v5, /device:TPU:14, one launch (start us, length us, event | category | flops | bytes accessed | tf_op | source)
XLA Modules:
  0.0 97.3 jit_solution(5366507631017835585)
XLA Ops:
  0.6 22.5 %line_sums.1 = (f32[2,8,256,256]{3,2,1,0:T(8,128)}, f32[2,8,256,256]{3,2,1,0:T(8,128)}) custom-call(s32[1,8,1280]{2,1,0:T(8,128)} %slots_in.1, s32[1,8,1280]{2,1,0:T(8,128)} %lines_in.1, s32[1,8]{1,0:T(1,128)} %counts.1, bf16[16384,256]{1,0:T(8,128)(2,1)} %acquired.1), custom_call_target="tpu_custom_call" | custom-call | tf_op jit(solution)/shard_map/line_sums/pallas_call | solution.py:121
  23.1 70.8 %reduce_smooth_return.1 = (bf16[1,256,256]{2,1,0:T(8,128)(2,1)}, bf16[8,128,256]{2,1,0:T(8,128)(2,1)}) custom-call(f32[2,8,256,256]{3,2,1,0:T(8,128)} %get-tuple-element.4.kept_sums, f32[2,8,256,256]{3,2,1,0:T(8,128)} %get-tuple-element.5.sent_sums, bf16[256,1024]{1,0:T(8,128)(2,1)} %stencil.1, s32[1,8,128]{2,1,0:T(8,128)} %read_ids.1, s32[1,8]{1,0:T(1,128)} %read_counts.1), custom_call_target="tpu_custom_call" | custom-call | tf_op jit(solution)/shard_map/reduce_smooth_return/pallas_call | solution.py:480
  93.9 1.6 %copy.11 = bf16[1,256,256]{2,1,0:T(8,128)(2,1)} copy(bf16[1,256,256]{2,1,0:T(8,128)(2,1)} %get-tuple-element.8) | data formatting | bytes 262144
  95.5 1.9 %copy.12 = bf16[8,128,256]{2,1,0:T(8,128)(2,1)} copy(bf16[8,128,256]{2,1,0:T(8,128)(2,1)} %get-tuple-element.9) | data formatting | bytes 1048576

commit v6 on v4

--- a/solution.py
+++ b/solution.py
@@ -84,21 +84,24 @@
     count = counts[0, tile]
     groups = count // UNROLL
 
-    def spot(ref, j):
-        return pl.ds(pl.multiple_of(ref[tile, j] * PARTS, PARTS), PARTS)
+    row_at = rows.reshape(rows.shape[0] // PARTS, PARTS, LANES)
+    even_at = even.reshape(even.shape[0] // PARTS, PARTS, LANES)
+    odd_at = odd.reshape(odd.shape[0] // PARTS, PARTS, LANES)
 
     @pl.loop(0, groups)
     def _(group):
         first = group * UNROLL
-        spots = [spot(lines, first + u) for u in range(UNROLL)]
-        added = [rows[spot(slots, first + u), :] for u in range(UNROLL)]
-        for u in range(UNROLL):
-            total = (even, odd)[u % 2]
-            total[spots[u], :] += added[u]
+        spots = [lines[tile, first + u] for u in range(UNROLL)]
+        added = [row_at[slots[tile, first + u]] for u in range(UNROLL)]
+        for u in range(0, UNROLL, 2):
+            first_sum = even_at[spots[u]] + added[u]
+            second_sum = odd_at[spots[u + 1]] + added[u + 1]
+            even_at[spots[u]] = first_sum
+            odd_at[spots[u + 1]] = second_sum
 
     @pl.loop(groups * UNROLL, count)
     def _(j):
-        even[spot(lines, j), :] += rows[spot(slots, j), :]
+        even_at[lines[tile, j]] += row_at[slots[tile, j]]
 
     core = lax.axis_index("cuts") % 2
     for x in range(kept_out.shape[0]):
@@ -238,7 +241,7 @@
     read_index = lax.broadcasted_iota(jnp.int32, (1, reads), 1)
     for t2 in range(tiles):
         wanted = jnp.where(read_index < read_counts[0, t2], read_ids[0, t2 : t2 + 1, :], -1)
-        chosen[t2] = jnp.where(field_lines == wanted, 1.0, 0.0).astype(jnp.bfloat16)
+        chosen[t2] = jnp.where(field_lines == wanted, 1.0, 0.0).T.astype(jnp.bfloat16)
 
     def pair(q_out, q_in, s_out, s_in, send, recv, at_out, at_in, device):
         return (
@@ -377,9 +380,8 @@
     field_out[0] = field
 
     def back(t2):
-        return lax.dot_general(
-            chosen[t2], field_out[0], (((0,), (0,)), ((), ())), preferred_element_type=jnp.float32
-        ).astype(jnp.bfloat16)
+        lines_read = jnp.dot(chosen[t2], field_out[0], preferred_element_type=jnp.float32)
+        return lines_read.astype(jnp.bfloat16)
 
     def copy5(s):
         return remote(
@@ -461,7 +463,7 @@
         scratch_shapes=[
             pltpu.VMEM((side, 2, spread, NY, NX), jnp.float32),
             pltpu.VMEM((side, 2, spread, NY, NX), jnp.float32),
-            pltpu.VMEM((tiles, NY, reads), jnp.bfloat16),
+            pltpu.VMEM((tiles, reads, NY), jnp.bfloat16),
             *coded(side - 1, 2, spread),
             *coded(2, side - 1, half),
             *coded(depth - 1),

time: 95.7 us -> 96.6 us (level)
  Pallas kernels: 89.7 us -> 91.3 us
    pallas_call x1, Pallas kernels: 61.8 us -> 67.2 us  [finish(): pl.pallas_call(field_kernel, out_shape=(jax.ShapeDtypeStruct((1, NY, NX),...]
    pallas_call x1, Pallas kernels: 27.9 us -> 24.1 us  [line_sums(): pl.pallas_call(line_sum_kernel, grid=(tile_count,), out_shape=(jax.ShapeD...]
where the time goes in v6:
time: 96.6 us; the launch traced here: 95.3 us
  Pallas kernels  91.3 us (95%)
  local copies, waits for them, and re-layouts  3.44 us (4%)
    pallas_call x1, Pallas kernels, finish(): pl.pallas_call(field_kernel, out_shape=(jax.ShapeDtypeStruct((1, NY, NX),...  67.2 us
    pallas_call x1, Pallas kernels, line_sums(): pl.pallas_call(line_sum_kernel, grid=(tile_count,), out_shape=(jax.ShapeD...  24.1 us
    unnamed x2, local copies, waits for them, and re-layouts  3.44 us

profile of v6, /device:TPU:14, one launch (start us, length us, event | category | flops | bytes accessed | tf_op | source)
XLA Modules:
  0.0 95.3 jit_solution(17233138740366174966)
XLA Ops:
  0.6 24.1 %line_sums.1 = (f32[2,8,256,256]{3,2,1,0:T(8,128)}, f32[2,8,256,256]{3,2,1,0:T(8,128)}) custom-call(s32[1,8,1280]{2,1,0:T(8,128)} %slots_in.1, s32[1,8,1280]{2,1,0:T(8,128)} %lines_in.1, s32[1,8]{1,0:T(1,128)} %counts.1, bf16[16384,256]{1,0:T(8,128)(2,1)} %acquired.1), custom_call_target="tpu_custom_call" | custom-call | tf_op jit(solution)/shard_map/line_sums/pallas_call | solution.py:122
  24.7 67.2 %reduce_smooth_return.1 = (bf16[1,256,256]{2,1,0:T(8,128)(2,1)}, bf16[8,128,256]{2,1,0:T(8,128)(2,1)}) custom-call(f32[2,8,256,256]{3,2,1,0:T(8,128)} %get-tuple-element.4.kept_sums, f32[2,8,256,256]{3,2,1,0:T(8,128)} %get-tuple-element.5.sent_sums, bf16[256,1024]{1,0:T(8,128)(2,1)} %stencil.1, s32[1,8,128]{2,1,0:T(8,128)} %read_ids.1, s32[1,8]{1,0:T(1,128)} %read_counts.1), custom_call_target="tpu_custom_call" | custom-call | tf_op jit(solution)/shard_map/reduce_smooth_return/pallas_call | solution.py:455
  91.9 1.6 %copy.11 = bf16[1,256,256]{2,1,0:T(8,128)(2,1)} copy(bf16[1,256,256]{2,1,0:T(8,128)(2,1)} %get-tuple-element.8) | data formatting | bytes 262144
  93.5 1.9 %copy.12 = bf16[8,128,256]{2,1,0:T(8,128)(2,1)} copy(bf16[8,128,256]{2,1,0:T(8,128)(2,1)} %get-tuple-element.9) | data formatting | bytes 1048576

commit v7 on v4

--- a/solution.py
+++ b/solution.py
@@ -10,7 +10,8 @@
 TAPS = 4
 ZDEV = 1
 LOAD_ROWS = 1024
-UNROLL = 8
+UNROLL = 32
+SPARE = 8
 LEVELS = 32767.0
 ROUNDER = 12582912.0
 WEIGHT = 0.15
@@ -84,21 +85,32 @@
     count = counts[0, tile]
     groups = count // UNROLL
 
-    def spot(ref, j):
-        return pl.ds(pl.multiple_of(ref[tile, j] * PARTS, PARTS), PARTS)
+    spare = even.shape[0] // PARTS - SPARE // PARTS
+
+    def spot(index):
+        return pl.ds(pl.multiple_of(index * PARTS, PARTS), PARTS)
+
+    def add_group(group, masked):
+        first = group * UNROLL
+        to = [lines[tile, first + u] for u in range(UNROLL)]
+        source = [slots[tile, first + u] for u in range(UNROLL)]
+        if masked:
+            to = [jnp.where(first + u < count, to[u], spare) for u in range(UNROLL)]
+            source = [jnp.where(first + u < count, source[u], 0) for u in range(UNROLL)]
+        added = [rows[spot(source[u]), :] for u in range(UNROLL)]
+        for u in range(0, UNROLL, 2):
+            first_sum = even[spot(to[u]), :] + added[u]
+            second_sum = odd[spot(to[u + 1]), :] + added[u + 1]
+            even[spot(to[u]), :] = first_sum
+            odd[spot(to[u + 1]), :] = second_sum
 
     @pl.loop(0, groups)
     def _(group):
-        first = group * UNROLL
-        spots = [spot(lines, first + u) for u in range(UNROLL)]
-        added = [rows[spot(slots, first + u), :] for u in range(UNROLL)]
-        for u in range(UNROLL):
-            total = (even, odd)[u % 2]
-            total[spots[u], :] += added[u]
-
-    @pl.loop(groups * UNROLL, count)
-    def _(j):
-        even[spot(lines, j), :] += rows[spot(slots, j), :]
+        add_group(group, False)
+
+    @pl.when(groups * UNROLL < count)
+    def _():
+        add_group(groups, True)
 
     core = lax.axis_index("cuts") % 2
     for x in range(kept_out.shape[0]):
@@ -114,6 +126,7 @@
     side = cut_count // 2
     rows_dev = acquired.shape[0]
     loads = rows_dev // LOAD_ROWS
+    assert slots.shape[2] % UNROLL == 0
     group_lines = cut_count * NY
     hbm = pl.BlockSpec(memory_space=pl.ANY)
     return pl.pallas_call(
@@ -131,8 +144,8 @@
         scratch_shapes=[
             pltpu.VMEM((rows_dev * PARTS, LANES), jnp.float32),
             pltpu.VMEM((loads, LOAD_ROWS, NX), jnp.bfloat16),
-            pltpu.VMEM((group_lines * PARTS, LANES), jnp.float32),
-            pltpu.VMEM((group_lines * PARTS, LANES), jnp.float32),
+            pltpu.VMEM((group_lines * PARTS + SPARE, LANES), jnp.float32),
+            pltpu.VMEM((group_lines * PARTS + SPARE, LANES), jnp.float32),
             pltpu.SMEM(slots.shape[1:], jnp.int32),
             pltpu.SMEM(lines.shape[1:], jnp.int32),
             pltpu.SemaphoreType.DMA((loads,)),

time: 95.7 us -> 98.1 us (1.025); the launches traced: 93.8 us -> 98.1 us
  Pallas kernels: 89.7 us -> 94 us
    pallas_call x1, Pallas kernels: 61.8 us -> 67.4 us  [finish(): pl.pallas_call(field_kernel, out_shape=(jax.ShapeDtypeStruct((1, NY, NX),...]
    pallas_call x1, Pallas kernels: 27.9 us -> 26.6 us  [line_sums(): pl.pallas_call(line_sum_kernel, grid=(tile_count,), out_shape=(jax.ShapeD...]
where the time goes in v7:
time: 98.1 us
  Pallas kernels  94 us (96%)
  local copies, waits for them, and re-layouts  3.44 us (4%)
    pallas_call x1, Pallas kernels, finish(): pl.pallas_call(field_kernel, out_shape=(jax.ShapeDtypeStruct((1, NY, NX),...  67.4 us
    pallas_call x1, Pallas kernels, line_sums(): pl.pallas_call(line_sum_kernel, grid=(tile_count,), out_shape=(jax.ShapeD...  26.6 us
    unnamed x2, local copies, waits for them, and re-layouts  3.44 us

profile of v7, /device:TPU:14, one launch (start us, length us, event | category | flops | bytes accessed | tf_op | source)
XLA Modules:
  0.0 98.1 jit_solution(3898676536089957021)
XLA Ops:
  0.6 26.6 %line_sums.1 = (f32[2,8,256,256]{3,2,1,0:T(8,128)}, f32[2,8,256,256]{3,2,1,0:T(8,128)}) custom-call(s32[1,8,1280]{2,1,0:T(8,128)} %slots_in.1, s32[1,8,1280]{2,1,0:T(8,128)} %lines_in.1, s32[1,8]{1,0:T(1,128)} %counts.1, bf16[16384,256]{1,0:T(8,128)(2,1)} %acquired.1), custom_call_target="tpu_custom_call" | custom-call | tf_op jit(solution)/shard_map/line_sums/pallas_call | solution.py:132
  27.3 67.4 %reduce_smooth_return.1 = (bf16[1,256,256]{2,1,0:T(8,128)(2,1)}, bf16[8,128,256]{2,1,0:T(8,128)(2,1)}) custom-call(f32[2,8,256,256]{3,2,1,0:T(8,128)} %get-tuple-element.4.kept_sums, f32[2,8,256,256]{3,2,1,0:T(8,128)} %get-tuple-element.5.sent_sums, bf16[256,1024]{1,0:T(8,128)(2,1)} %stencil.1, s32[1,8,128]{2,1,0:T(8,128)} %read_ids.1, s32[1,8]{1,0:T(1,128)} %read_counts.1), custom_call_target="tpu_custom_call" | custom-call | tf_op jit(solution)/shard_map/reduce_smooth_return/pallas_call | solution.py:466
  94.7 1.6 %copy.11 = bf16[1,256,256]{2,1,0:T(8,128)(2,1)} copy(bf16[1,256,256]{2,1,0:T(8,128)(2,1)} %get-tuple-element.8) | data formatting | bytes 262144
  96.3 1.9 %copy.12 = bf16[8,128,256]{2,1,0:T(8,128)(2,1)} copy(bf16[8,128,256]{2,1,0:T(8,128)(2,1)} %get-tuple-element.9) | data formatting | bytes 1048576
